TPU v7x, 256 devices: a whole 4x4x8 slice. The times are simulated.
256 devices in a mesh: dp: 32 (over x, z_hi, core), tensor: 8 (over y, z_lo).
Axes of the slice: x: 4, y: 4, z: 8 (z_hi: 4, z_lo: 2; z = z_hi * 2 + z_lo), core: 2. Of those that a mesh axis runs over, the one named last changes fastest.
Arguments:
- inputs: bfloat16 [20480, 4096], P(('dp', 'tensor')), may hold values from -8 to 8
- projections: bfloat16 [3, 4096, 2048], P(None, 'dp', 'tensor'), may hold values from -0.0625 to 0.0625
- upstream_grad: bfloat16 [20480, 2048], P('dp', 'tensor'), may hold values from -6 to 6
Outputs:
- input_grad: bfloat16 [20480, 4096], P(('dp', 'tensor'))
- weight_grad: float32 [3, 4096, 2048], P(None, 'dp', 'tensor')
All inputs are finite; a program needn't handle non-finite values.
Results may differ from a plain program's by a relative error of at most 0.035.
Values may be sent and summed in bfloat16 or wider, within the bound.
A program may use at most 64 MiB of HBM per device.

v0:
```python
import jax
import jax.numpy as jnp
from jax import lax
from jax.sharding import PartitionSpec as P

HS = 128


def rotate(field, sign):
    half_size = HS // 2
    position = jnp.arange(field.shape[0], dtype=jnp.float32)
    frequency = 10000.0 ** (-jnp.arange(half_size, dtype=jnp.float32) / half_size)
    angles = position[:, None] * frequency[None, :]
    cosine = jnp.cos(angles)[:, None, :]
    sine_part = jnp.sin(angles)[:, None, :]
    first = field[..., :half_size]
    second = field[..., half_size:]
    return jnp.concatenate(
        [first * cosine - sign * second * sine_part, second * cosine + sign * first * sine_part], -1
    )


def attend(projected, grad_out):
    length = projected.shape[1]
    heads_here = projected.shape[2] // HS
    score_scale = HS ** (-0.5)
    f32 = jnp.float32
    queries = rotate(projected[0].reshape(length, heads_here, HS), 1.0).astype(jnp.bfloat16)
    keys_rot = rotate(projected[1].reshape(length, heads_here, HS), 1.0).astype(jnp.bfloat16)
    values = projected[2].reshape(length, heads_here, HS).astype(jnp.bfloat16)
    scores = jnp.einsum("shd,thd->hst", queries, keys_rot, preferred_element_type=f32) * score_scale
    causal = jnp.arange(length)[:, None] >= jnp.arange(length)[None, :]
    scores = jnp.where(causal[None], scores, -1e30)
    raised = jnp.exp(scores - jnp.max(scores, -1, keepdims=True))
    probability = raised / jnp.sum(raised, -1, keepdims=True)
    probability_low = probability.astype(jnp.bfloat16)
    attended = jnp.einsum("hst,thd->shd", probability_low, values, preferred_element_type=f32)
    upstream = grad_out.reshape(length, heads_here, HS)
    grad_values = jnp.einsum(
        "hst,shd->thd", probability_low, upstream, preferred_element_type=f32
    ).astype(jnp.bfloat16)
    grad_probs = jnp.einsum("shd,thd->hst", upstream, values, preferred_element_type=f32)
    row_dots = jnp.transpose(jnp.sum(upstream.astype(f32) * attended, -1))
    grad_scores = (probability * (grad_probs - row_dots[:, :, None]) * score_scale).astype(
        jnp.bfloat16
    )
    grad_queries = jnp.einsum("hst,thd->shd", grad_scores, keys_rot, preferred_element_type=f32)
    grad_keys = jnp.einsum("hst,shd->thd", grad_scores, queries, preferred_element_type=f32)
    grad_queries = rotate(grad_queries, -1.0).astype(jnp.bfloat16)
    grad_keys = rotate(grad_keys, -1.0).astype(jnp.bfloat16)
    return jnp.stack([grad_queries, grad_keys, grad_values]).reshape(3, length, heads_here * HS)


def shards(inputs, projections, upstream_grad):
    f32 = jnp.float32
    full_x = lax.all_gather(inputs, "tensor", axis=0, tiled=True)
    projected = jnp.einsum(
        "sd,jdh->jsh",
        full_x,
        lax.all_gather(projections, "dp", axis=1, tiled=True),
        preferred_element_type=f32,
    )
    grads = attend(projected, upstream_grad)
    x_partial = jnp.einsum(
        "jsh,jdh->sd",
        grads,
        lax.all_gather(projections, "dp", axis=1, tiled=True),
        preferred_element_type=f32,
    )
    input_grad = lax.psum_scatter(
        x_partial.astype(jnp.bfloat16), "tensor", scatter_dimension=0, tiled=True
    )
    w_partial = jnp.einsum("sd,jsh->jdh", full_x, grads, preferred_element_type=f32)
    weight_grad = lax.psum_scatter(
        w_partial.astype(jnp.bfloat16), "dp", scatter_dimension=1, tiled=True
    ).astype(jnp.float32)
    return (input_grad, weight_grad)


def solution(mesh):
    return jax.shard_map(
        shards,
        mesh=mesh,
        in_specs=(P(("dp", "tensor"), None), P(None, "dp", "tensor"), P("dp", "tensor")),
        out_specs=(P(("dp", "tensor"), None), P(None, "dp", "tensor")),
        check_vma=False,
    )
```

profile of v0, /device:TPU:1, one launch (start us, length us, event | category | flops | bytes accessed | tf_op | source)
XLA Modules:
  0.0 487.2 jit_solution(1952278342249810811)
XLA Ops:
  7.2 0.7 all-gather.5.cloned.1.call-update
  7.9 1.7 copy.49
  9.8 1.9 copy.54
  11.6 0.9 iota_compare_fusion
  12.5 1.9 broadcast_multiply_fusion
  14.4 111.6 %all-gather.5.cloned.1.call-done = bf16[640,4096]{1,0:T(8,128)(2,1)} async-done(((bf16[80,4096]{1,0:T(8,128)(2,1)}), bf16[640,4096]{1,0:T(8,128)(2,1)}) %all-gather.5.cloned.1.call-update) | async-done | bytes 5242896 | tf_op jit(solution)/shard_map/all_gather | solution.py:56
  126.0 78.4 %all-gather.3.cloned.1.call-done = bf16[3,4096,256]{1,2,0:T(8,128)(2,1)} async-done(((bf16[3,128,256]{1,2,0:T(8,128)(2,1)}), bf16[3,4096,256]{1,2,0:T(8,128)(2,1)}) %all-gather.3.cloned.1.call-update) | async-done | bytes 6291472 | tf_op jit(solution)/shard_map/all_gather | solution.py:60
  204.4 8.8 %fusion.11 = f32[3,640,256]{1,2,0:T(8,128)S(1)} fusion(bf16[3,4096,256]{1,2,0:T(8,128)(2,1)} %all-gather.3.cloned.1.call-done, bf16[640,4096]{1,0:T(8,128)(2,1)} %all-gather.5.cloned.1.call-done), kind=kOutput, calls=%fused_computation.18 | convolution fusion | flops 4026531840 | bytes 13500416 | tf_op jit(solution)/shard_map/sd,jdh->jsh/dot_general | solution.py:57
  213.2 0.8 slice.81
  214.0 0.8 fusion.31
  215.1 0.2 copy.90
  215.3 0.2 copy.87
  215.6 1.2 copy.89
  216.8 1.3 subtract_convert_fusion.3
  218.1 3.0 fusion.32
  221.1 0.3 fusion.14
  221.4 0.7 copy-done.2
  222.1 1.3 convolution_convert_fusion.1
  223.4 0.5 fusion.16
  224.0 0.7 fusion.6
  225.0 0.6 convolution_bitcast_fusion
  225.7 1.0 convolution_bitcast_fusion.1
  226.9 0.5 fusion.17
  227.4 0.4 pad_maximum_fusion.5
  228.5 9.7 %fusion.1 = bf16[3,4096,256]{1,2,0:T(8,128)(2,1)} fusion(bf16[640,4096]{1,0:T(8,128)(2,1)} %all-gather.5.cloned.1.call-done, bf16[1,640,256]{2,1,0:T(8,128)(2,1)S(1)} %copy.69, bf16[1,640,256]{2,1,0:T(8,128)(2,1)S(1)} %copy.68, bf16[1,640,256]{2,1,0:T(8,128)(2,1)S(1)} %copy.67), kind=kOutput, calls=%fused_computation.3 | convolution fusion | flops 4030660608 | bytes 12517376 | tf_op jit(solution)/shard_map/sd,jsh->jdh/dot_general | solution.py:73
  238.2 13.1 %copy.85 = bf16[3,4096,256]{2,0,1:T(4,128)(2,1)} copy(bf16[3,4096,256]{1,2,0:T(8,128)(2,1)} %fusion.1) | data formatting | bytes 12582912
  251.4 7.8 %copy.91 = bf16[512,8,3,256]{3,1,2,0:T(8,128)(2,1)} copy(bf16[512,8,3,256]{3,2,1,0:T(4,128)(2,1)} %bitcast.62) | data formatting | bytes 12582912
  259.3 8.7 %bitcast_convert_fusion = bf16[640,4096]{1,0:T(8,128)(2,1)} fusion(bf16[3,4096,256]{1,2,0:T(8,128)(2,1)} %all-gather.3.cloned.1.call-done, bf16[1,640,256]{2,1,0:T(8,128)(2,1)S(1)} %copy.69, bf16[1,640,256]{2,1,0:T(8,128)(2,1)S(1)} %copy.68, bf16[1,640,256]{2,1,0:T(8,128)(2,1)S(1)} %copy.67), kind=kOutput, calls=%fused_computation.1 | convolution fusion | flops 4030136320 | bytes 12517376 | tf_op jit(solution)/shard_map/jsh,jdh->sd/dot_general | solution.py:64
  268.0 97.8 %reduce-scatter.7.cloned.1.call-done = bf16[128,768]{1,0:T(8,128)(2,1)} async-done(((bf16[4096,768]{1,0:T(8,128)(2,1)}), bf16[128,768]{1,0:T(8,128)(2,1)}) %reduce-scatter.7.cloned.1.call-update) | async-done | bytes 196624
  365.8 1.0 reshape.102
  367.1 0.9 copy.72
  368.0 112.7 %reduce-scatter.5.cloned.1.call-done = bf16[80,4096]{1,0:T(8,128)(2,1)} async-done(((bf16[640,4096]{1,0:T(8,128)(2,1)}), bf16[80,4096]{1,0:T(8,128)(2,1)}) %reduce-scatter.5.cloned.1.call-update) | async-done | bytes 655376 | tf_op jit(solution)/shard_map/reduce_scatter | solution.py:70
  (36 shorter events, 2.1 us)
Async XLA Ops:
  7.2 118.9 %all-gather.5.cloned.1.call-start = ((), (), s32[]{:S(2)}) async-start(), calls=%async_computation.3 | async-start | bytes 5898240 | tf_op jit(solution)/shard_map/all_gather | solution.py:56
  7.9 196.5 %all-gather.3.cloned.1.call-start = ((), (), s32[]{:S(2)}) async-start(), calls=%async_computation.2 | async-start | bytes 6488064 | tf_op jit(solution)/shard_map/all_gather | solution.py:60
  9.7 356.1 %reduce-scatter.7.cloned.1.call-start = ((), (), s32[]{:S(2)}) async-start(), calls=%async_computation.5 | async-start | bytes 6488064
  14.4 202.4 %copy-start = (f32[640,64]{1,0:T(8,128)}, f32[640,64]{1,0:T(8,128)S(1)}, u32[]{:S(2)}) copy-start(f32[640,64]{1,0:T(8,128)S(1)} %get-tuple-element.28) | copy-start | bytes 491524
  221.1 1.0 copy-start.2
  221.1 2.3 copy-start.9
  223.9 1.0 copy-start.6
  223.9 1.1 copy-start.7
  223.9 1.7 copy-start.4
  224.0 1.7 copy-start.5
  225.0 1.6 copy-start.8
  225.0 1.8 copy-start.1
  225.0 1.8 copy-start.3
  259.2 221.4 %reduce-scatter.5.cloned.1.call-start = ((), (), s32[]{:S(2)}) async-start(), calls=%async_computation.4 | async-start | bytes 5898240 | tf_op jit(solution)/shard_map/reduce_scatter | solution.py:70
Sparse Core Ops, SparseCore 0:
  9.8 116.2 all-gather.4
  128.5 75.8 all-gather.2
  259.3 106.4 reduce-scatter.6
  369.0 111.5 reduce-scatter.4
where the time goes:
time: 488 us; the launch traced here: 487 us
  waiting for transfers between devices  401 us (82%)
  matrix products  34.4 us (7%)
  local copies, waits for them, and re-layouts  32.2 us (7%)
  between operations  14 us (3%)
  other arithmetic  5.26 us (1%)
    reduce_scatter x1, waiting for transfers between devices, shards(): lax.psum_scatter(x_partial.astype(jnp.bfloat16), 'tensor', scatter_dimens...  113 us
    all_gather x1, waiting for transfers between devices, shards(): full_x = lax.all_gather(inputs, 'tensor', axis=0, tiled=True)  112 us
    unnamed x5, waiting for transfers between devices  98.5 us
    all_gather x1, waiting for transfers between devices, shards(): lax.all_gather(projections, 'dp', axis=1, tiled=True)  78.4 us
    unnamed x31, local copies, waits for them, and re-layouts  29.6 us
  transfers between devices with their start and end apart: 4, of which 4 were waited for; matrix products, arithmetic and copies ran while one was open for 4% of the time, Pallas kernels for 0%

commit v1 on v0

v1 whole, which is shorter than its diff:
```python
import functools

import jax
import jax.numpy as jnp
import numpy as np
from jax import lax
from jax.experimental import pallas as pl
from jax.experimental.pallas import tpu as pltpu
from jax.sharding import PartitionSpec as P

HS = 128
SEQ = 640
D = 4096
MESH = pl.DeviceIdType.MESH
F32 = jnp.float32
BF16 = jnp.bfloat16
HALF = D // 2


def rotary_tables():
    half = HS // 2
    frequency = 10000.0 ** (-np.arange(half, dtype=np.float64) / half)
    angles = np.arange(SEQ, dtype=np.float64)[:, None] * frequency[None, :]
    cosine, sine = np.cos(angles), np.sin(angles)
    return (
        np.concatenate([cosine, cosine], -1).astype(np.float32),
        np.concatenate([-sine, sine], -1).astype(np.float32),
    )


def dot_nn(a, b):
    return lax.dot_general(a, b, (((1,), (0,)), ((), ())), preferred_element_type=F32)


def dot_nt(a, b):
    return lax.dot_general(a, b, (((1,), (1,)), ((), ())), preferred_element_type=F32)


def dot_tn(a, b):
    return lax.dot_general(a, b, (((0,), (0,)), ((), ())), preferred_element_type=F32)


N_SEND = 64
N_RECV = 64


def kernel(
    x_in, w_in, up_in, cos_in, sin_in, dx_out, dw_out,
    xv, wv, upv, cosv, sinv, qkv, gv, accv, dxp, dwp,
    rel_v, fin_v, zl_v, sib_v, xrel_v, xfin_v, zrel_v, zfin_v,
    send_sem, recv_sem, local_sem,
):
    dp = lax.axis_index("dp")
    tensor = lax.axis_index("tensor")
    x, zh, c = dp // 8, (dp // 2) % 4, dp % 2
    y, zl = tensor // 2, tensor % 2

    def place(xx, zz, cc, yy, ll):
        return {"dp": xx * 8 + zz * 2 + cc, "tensor": yy * 2 + ll}

    def ring(v, step):
        return lax.rem(v + (step + 4), 4)

    yp, ym = place(x, zh, c, ring(y, 1), zl), place(x, zh, c, ring(y, -1), zl)
    xp, xm = place(ring(x, 1), zh, c, y, zl), place(ring(x, -1), zh, c, y, zl)
    zp, zm = place(x, ring(zh, 1), c, y, zl), place(x, ring(zh, -1), c, y, zl)
    mate = place(x, zh, c, y, 1 - zl)
    sibling = place(x, zh, 1 - c, y, zl)
    everyone = (yp, ym, xp, xm, zp, zm, mate, sibling)

    keys = {}
    sends = []

    def key_index(key):
        return keys.setdefault(key, len(keys))

    def send(src, dst, key, device):
        copy = pltpu.make_async_remote_copy(
            src_ref=src, dst_ref=dst, send_sem=send_sem.at[len(sends)],
            recv_sem=recv_sem.at[key_index(key)], device_id=device, device_id_type=MESH,
        )
        copy.start()
        sends.append(copy)

    def recv(dst, key, device):
        pltpu.make_async_remote_copy(
            src_ref=dst, dst_ref=dst, send_sem=send_sem.at[0],
            recv_sem=recv_sem.at[key_index(key)], device_id=device, device_id_type=MESH,
        ).wait_recv()

    def rows(yy, ll):
        return pl.ds(pl.multiple_of(yy * 160 + ll * 80, 16), 80)

    def cols(h):
        return pl.ds(h * HALF, HALF)

    own_x = xv.at[rows(y, zl)]

    def unit(xx, zz):
        return wv.at[:, xx * 4 + zz, c]

    locals_ = [
        pltpu.make_async_copy(x_in, own_x, local_sem.at[0]),
        pltpu.make_async_copy(w_in, unit(x, zh), local_sem.at[1]),
        pltpu.make_async_copy(up_in, upv, local_sem.at[2]),
        pltpu.make_async_copy(cos_in, cosv, local_sem.at[3]),
        pltpu.make_async_copy(sin_in, sinv, local_sem.at[4]),
    ]
    for copy in locals_:
        copy.start()

    barrier = pltpu.get_barrier_semaphore()
    for device in everyone:
        pl.semaphore_signal(barrier, inc=1, device_id=device, device_id_type=MESH)
    pl.semaphore_wait(barrier, len(everyone))

    send(x_in, own_x, "Xp", mate)
    send(w_in, unit(x, zh), ("W", 0, -1), zp)
    send(w_in, unit(x, zh), ("W", 0, 1), zm)
    send(x_in, own_x, ("Xo", -1), yp)
    send(x_in, own_x, ("Xo", 1), ym)
    send(w_in, unit(x, zh), ("W", -1, 0), xp)
    send(w_in, unit(x, zh), ("W", 1, 0), xm)
    for copy in locals_:
        copy.wait()

    top, bottom = pl.ds(0, 64), pl.ds(64, 64)

    def unit_half(xx, zz, part):
        return wv.at[:, xx * 4 + zz, c, part]

    def group(xx, cc):
        return wv.at[:, pl.ds(xx * 4, 4), cc]

    xn, xq, x2 = ring(x, -1), ring(x, 1), ring(x, 2)
    zn, zq, z2 = ring(zh, -1), ring(zh, 1), ring(zh, 2)
    yn, yq, y2 = ring(y, -1), ring(y, 1), ring(y, 2)

    recv(unit(x, zn), ("W", 0, -1), zm)
    send(unit_half(x, zn, top), unit_half(x, zn, top), "WrA", zp)
    send(unit(x, zn), unit(x, zn), ("W", -1, -1), xp)
    send(unit(x, zn), unit(x, zn), ("W", 1, -1), xm)
    recv(unit(x, zq), ("W", 0, 1), zp)
    send(unit_half(x, zq, bottom), unit_half(x, zq, bottom), "WrB", zm)
    send(unit(x, zq), unit(x, zq), ("W", -1, 1), xp)
    send(unit(x, zq), unit(x, zq), ("W", 1, 1), xm)

    recv(unit(xn, zh), ("W", -1, 0), xm)
    send(unit(xn, zh), unit(xn, zh), ("W", 2, 0), xp)
    recv(unit(xq, zh), ("W", 1, 0), xp)

    own, other = rows(y, zl), rows(y, 1 - zl)
    recv(xv.at[other], "Xp", mate)
    send(xv.at[other], xv.at[other], ("Xq", -1), yp)
    send(xv.at[other], xv.at[other], ("Xq", 1), ym)
    blk = rows(yn, zl)
    recv(xv.at[blk], ("Xo", -1), ym)
    send(xv.at[blk, cols(0)], xv.at[blk, cols(0)], ("Xr", 0, 0), yp)
    blk = rows(yq, zl)
    recv(xv.at[blk], ("Xo", 1), yp)
    send(xv.at[blk, cols(1)], xv.at[blk, cols(1)], ("Xr", 0, 1), ym)

    recv(unit_half(x, z2, top), "WrA", zm)
    recv(unit_half(x, z2, bottom), "WrB", zp)
    send(unit(x, z2), unit(x, z2), ("W", -1, 2), xp)
    send(unit(x, z2), unit(x, z2), ("W", 1, 2), xm)
    send(group(x, c), group(x, c), ("S", 0), sibling)

    recv(unit(xn, zn), ("W", -1, -1), xm)
    send(unit(xn, zn), unit(xn, zn), ("W", 2, -1), xp)
    recv(unit(xq, zq), ("W", 1, 1), xp)
    send(unit(xq, zq), unit(xq, zq), ("W", 2, 1), xm)
    recv(unit(xq, zn), ("W", 1, -1), xp)
    recv(unit(xn, zq), ("W", -1, 1), xm)
    recv(unit(xq, z2), ("W", 1, 2), xp)
    send(unit(xq, z2), unit(xq, z2), ("W", 2, 2), xm)
    recv(unit(xn, z2), ("W", -1, 2), xm)
    send(group(xn, c), group(xn, c), ("S", -1), sibling)
    send(group(xq, c), group(xq, c), ("S", 1), sibling)

    blk = rows(yn, 1 - zl)
    recv(xv.at[blk], ("Xq", -1), ym)
    send(xv.at[blk, cols(0)], xv.at[blk, cols(0)], ("Xr", 1, 0), yp)
    blk = rows(yq, 1 - zl)
    recv(xv.at[blk], ("Xq", 1), yp)
    send(xv.at[blk, cols(1)], xv.at[blk, cols(1)], ("Xr", 1, 1), ym)

    recv(unit(x2, zh), ("W", 2, 0), xm)
    recv(unit(x2, zn), ("W", 2, -1), xm)
    recv(unit(x2, zq), ("W", 2, 1), xp)
    recv(unit(x2, z2), ("W", 2, 2), xp)
    send(group(x2, c), group(x2, c), ("S", 2), sibling)
    recv(group(x, 1 - c), ("S", 0), sibling)
    recv(group(xn, 1 - c), ("S", -1), sibling)
    recv(group(xq, 1 - c), ("S", 1), sibling)
    recv(group(x2, 1 - c), ("S", 2), sibling)

    def project(yy):
        r = pl.ds(pl.multiple_of(yy * 160, 32), 160)
        cosine, sine = cosv[r], sinv[r]

        @pl.loop(0, 3)
        def _(j):
            p = dot_nn(xv[r], wv[j].reshape(D, 256))
            rotated = j < 2
            cc = jnp.where(rotated, cosine, 1.0)
            ss = jnp.where(rotated, sine, 0.0)
            for h in range(2):
                ph = p[:, h * HS:(h + 1) * HS]
                qkv[j, h, r] = (ph * cc + pltpu.roll(ph, 64, 1) * ss).astype(BF16)

    project(y)
    project(yn)
    project(yq)
    recv(xv.at[rows(y2, zl), cols(0)], ("Xr", 0, 0), ym)
    recv(xv.at[rows(y2, zl), cols(1)], ("Xr", 0, 1), yp)
    recv(xv.at[rows(y2, 1 - zl), cols(0)], ("Xr", 1, 0), ym)
    recv(xv.at[rows(y2, 1 - zl), cols(1)], ("Xr", 1, 1), yp)
    project(y2)

    scale = HS ** -0.5
    lower = lax.broadcasted_iota(jnp.int32, (128, 128), 0) >= lax.broadcasted_iota(
        jnp.int32, (128, 128), 1
    )

    def rotate_back(v, r):
        return (v * cosv[r] - pltpu.roll(v, 64, 1) * sinv[r]).astype(BF16)

    for h in range(2):
        hc = pl.ds(h * HS, HS)
        for i in reversed(range(5)):
            n = (i + 1) * 128
            r = pl.ds(i * 128, 128)
            head = pl.ds(0, n)
            q, k, v = qkv[0, h, r], qkv[1, h, head], qkv[2, h, head]
            up = upv[r, hc]
            s = dot_nt(q, k) * scale
            diagonal = jnp.where(lower, s[:, i * 128:], -1e30)
            s = diagonal if i == 0 else jnp.concatenate([s[:, : i * 128], diagonal], 1)
            e = jnp.exp(s - jnp.max(s, 1, keepdims=True))
            prob = e / jnp.sum(e, 1, keepdims=True)
            low = prob.astype(BF16)
            gp = dot_nt(up, v)
            att = dot_nn(low, v)
            dots = jnp.sum(up.astype(F32) * att, 1, keepdims=True)
            gs = (prob * (gp - dots) * scale).astype(BF16)
            gv[r, pl.ds(h * HS, HS)] = rotate_back(dot_nn(gs, k), r)
            dk, dv = dot_tn(gs, q), dot_tn(low, up)
            if i == 4:
                accv[0], accv[1] = dk, dv
            else:
                accv[0, head] += dk
                accv[1, head] += dv
        full = pl.ds(0, SEQ)
        gv[:, pl.ds(256 + h * HS, HS)] = rotate_back(accv[0], full)
        gv[:, pl.ds(512 + h * HS, HS)] = accv[1].astype(BF16)

    def x_term(yy):
        r = pl.ds(pl.multiple_of(yy * 160, 32), 160)

        @pl.loop(0, 4)
        def _(i):
            total = None
            for j in range(3):
                w = wv[j, pl.ds(i * 4, 4)].reshape(1024, 256)
                t = dot_nt(gv[r, pl.ds(j * 256, 256)], w)
                total = t if total is None else total + t
            dxp[r, pl.ds(pl.multiple_of(i * 1024, 1024), 1024)] = total.astype(BF16)

    def w_term(xx):
        @pl.loop(0, 4)
        def _(i):
            b = xx * 4 + i
            t = dot_tn(xv[:, pl.ds(pl.multiple_of(b * 256, 256), 256)], gv[...])
            for cc in range(2):
                for j in range(3):
                    dwp[b, cc, j] = t[cc * 128:(cc + 1) * 128, j * 256:(j + 1) * 256].astype(BF16)

    def add_into(dst, src):
        dst[...] = (dst[...].astype(F32) + src[...].astype(F32)).astype(BF16)

    def xpart(yy, dz, h):
        return dxp.at[rows(yy, zl if dz == 0 else 1 - zl), cols(h)]

    def wgroup(xx, cc, first=0, count=4):
        return dwp.at[pl.ds(xx * 4 + first, count), cc]

    def send_sib(xx, dx):
        send(wgroup(xx, 1 - c), sib_v.at[pl.ds(xx * 4, 4)], ("DS", dx), sibling)

    def recv_sib(xx, dx):
        recv(sib_v.at[pl.ds(xx * 4, 4)], ("DS", dx), sibling)

        @pl.loop(0, 4)
        def _(i):
            add_into(dwp.at[xx * 4 + i, c], sib_v.at[xx * 4 + i])

    x_term(y2)
    for dz in (1, 0):
        send(xpart(y2, dz, 0), rel_v.at[0, dz], ("R", 0, dz), yp)
        send(xpart(y2, dz, 1), rel_v.at[1, dz], ("R", 1, dz), ym)
    w_term(x2)
    send_sib(x2, 2)
    x_term(yq)
    send(xpart(yq, 1, 1), fin_v.at[0, 1, 1], ("F", 0, 1, 1), yp)
    x_term(yn)
    send(xpart(yn, 1, 0), fin_v.at[1, 1, 0], ("F", 1, 1, 0), ym)
    recv_sib(x2, 2)
    send(wgroup(x2, c, 0, 2), xrel_v.at[0], ("XR", 0), xp)
    send(wgroup(x2, c, 2, 2), xrel_v.at[1], ("XR", 1), xm)
    w_term(xq)
    send_sib(xq, 1)
    w_term(xn)
    send_sib(xn, -1)
    for dz in (1, 0):
        if dz == 0:
            send(xpart(yq, 0, 1), fin_v.at[0, 0, 1], ("F", 0, 0, 1), yp)
            send(xpart(yn, 0, 0), fin_v.at[1, 0, 0], ("F", 1, 0, 0), ym)
        recv(rel_v.at[0, dz], ("R", 0, dz), ym)
        add_into(xpart(yq, dz, 0), rel_v.at[0, dz])
        send(xpart(yq, dz, 0), fin_v.at[0, dz, 0], ("F", 0, dz, 0), yp)
        recv(rel_v.at[1, dz], ("R", 1, dz), yp)
        add_into(xpart(yn, dz, 1), rel_v.at[1, dz])
        send(xpart(yn, dz, 1), fin_v.at[1, dz, 1], ("F", 1, dz, 1), ym)
    recv_sib(xq, 1)
    send(wgroup(xq, c, 2, 2), xfin_v.at[0, pl.ds(2, 2)], ("XF", 0, 2), xp)
    recv_sib(xn, -1)
    send(wgroup(xn, c, 0, 2), xfin_v.at[1, pl.ds(0, 2)], ("XF", 1, 0), xm)
    x_term(y)
    w_term(x)
    send_sib(x, 0)
    recv(xrel_v.at[0], ("XR", 0), xm)
    for i in range(2):
        add_into(dwp.at[xq * 4 + i, c], xrel_v.at[0, i])
    send(wgroup(xq, c, 0, 2), xfin_v.at[0, pl.ds(0, 2)], ("XF", 0, 0), xp)
    recv(xrel_v.at[1], ("XR", 1), xp)
    for i in range(2):
        add_into(dwp.at[xn * 4 + 2 + i, c], xrel_v.at[1, i])
    send(wgroup(xn, c, 2, 2), xfin_v.at[1, pl.ds(2, 2)], ("XF", 1, 2), xm)
    recv_sib(x, 0)

    for h in (1, 0):
        recv(fin_v.at[0, 1, h], ("F", 0, 1, h), ym)
        recv(fin_v.at[1, 1, h], ("F", 1, 1, h), yp)
        part = xpart(y, 1, h)
        part[...] = (
            part[...].astype(F32) + fin_v[0, 1, h].astype(F32) + fin_v[1, 1, h].astype(F32)
        ).astype(BF16)
        send(part, zl_v.at[h], ("Z", h), mate)

    for first in (2, 0):
        recv(xfin_v.at[0, pl.ds(first, 2)], ("XF", 0, first), xm)
    for first in (0, 2):
        recv(xfin_v.at[1, pl.ds(first, 2)], ("XF", 1, first), xp)

    @pl.loop(0, 4)
    def _(i):
        dst = dwp.at[x * 4 + i, c]
        dst[...] = (
            dst[...].astype(F32) + xfin_v[0, i].astype(F32) + xfin_v[1, i].astype(F32)
        ).astype(BF16)

    def wz(zz):
        return dwp.at[x * 4 + zz, c]

    def wz_half(zz, part):
        return dwp.at[x * 4 + zz, c, :, part]

    send(wz_half(z2, top), zrel_v.at[0], ("ZR", 0), zp)
    send(wz_half(z2, bottom), zrel_v.at[1], ("ZR", 1), zm)
    send(wz_half(zq, bottom), zfin_v.at[0, :, bottom], ("ZF", 0, 1), zp)
    send(wz_half(zn, top), zfin_v.at[1, :, top], ("ZF", 1, 0), zm)
    recv(zrel_v.at[0], ("ZR", 0), zm)
    add_into(wz_half(zq, top), zrel_v.at[0])
    send(wz_half(zq, top), zfin_v.at[0, :, top], ("ZF", 0, 0), zp)
    recv(zrel_v.at[1], ("ZR", 1), zp)
    add_into(wz_half(zn, bottom), zrel_v.at[1])
    send(wz_half(zn, bottom), zfin_v.at[1, :, bottom], ("ZF", 1, 1), zm)

    for h in (1, 0):
        recv(fin_v.at[0, 0, h], ("F", 0, 0, h), ym)
        recv(fin_v.at[1, 0, h], ("F", 1, 0, h), yp)
        recv(zl_v.at[h], ("Z", h), mate)
        dx_out[:, h * HALF:(h + 1) * HALF] = (
            xpart(y, 0, h)[...].astype(F32)
            + fin_v[0, 0, h].astype(F32)
            + fin_v[1, 0, h].astype(F32)
            + zl_v[h].astype(F32)
        ).astype(BF16)

    recv(zfin_v.at[0, :, bottom], ("ZF", 0, 1), zm)
    recv(zfin_v.at[0, :, top], ("ZF", 0, 0), zm)
    recv(zfin_v.at[1, :, top], ("ZF", 1, 0), zp)
    recv(zfin_v.at[1, :, bottom], ("ZF", 1, 1), zp)
    dw_out[...] = wz(zh)[...].astype(F32) + zfin_v[0].astype(F32) + zfin_v[1].astype(F32)

    for copy in sends:
        copy.wait_send()
    assert len(sends) <= N_SEND and len(keys) <= N_RECV


def shards(inputs, projections, upstream_grad):
    cosine, sine = rotary_tables()
    any_spec = pl.BlockSpec(memory_space=pl.ANY)
    vmem = pl.BlockSpec(memory_space=pltpu.VMEM)
    return pl.pallas_call(
        kernel,
        out_shape=(
            jax.ShapeDtypeStruct((80, D), BF16),
            jax.ShapeDtypeStruct((3, 128, 256), F32),
        ),
        in_specs=[any_spec] * 5,
        out_specs=(vmem, vmem),
        scratch_shapes=[
            pltpu.VMEM((SEQ, D), BF16),
            pltpu.VMEM((3, 16, 2, 128, 256), BF16),
            pltpu.VMEM((SEQ, 256), BF16),
            pltpu.VMEM((SEQ, HS), F32),
            pltpu.VMEM((SEQ, HS), F32),
            pltpu.VMEM((3, 2, SEQ, HS), BF16),
            pltpu.VMEM((SEQ, 768), BF16),
            pltpu.VMEM((2, SEQ, HS), F32),
            pltpu.VMEM((SEQ, D), BF16),
            pltpu.VMEM((16, 2, 3, 128, 256), BF16),
            pltpu.VMEM((2, 2, 80, HALF), BF16),
            pltpu.VMEM((2, 2, 2, 80, HALF), BF16),
            pltpu.VMEM((2, 80, HALF), BF16),
            pltpu.VMEM((16, 3, 128, 256), BF16),
            pltpu.VMEM((2, 2, 3, 128, 256), BF16),
            pltpu.VMEM((2, 4, 3, 128, 256), BF16),
            pltpu.VMEM((2, 3, 64, 256), BF16),
            pltpu.VMEM((2, 3, 128, 256), BF16),
            pltpu.SemaphoreType.DMA((N_SEND,)),
            pltpu.SemaphoreType.DMA((N_RECV,)),
            pltpu.SemaphoreType.DMA((5,)),
        ],
        compiler_params=pltpu.CompilerParams(
            collective_id=0, has_side_effects=True, vmem_limit_bytes=60 * 2**20
        ),
        name="mixer_backward",
    )(inputs, projections, upstream_grad, jnp.asarray(cosine), jnp.asarray(sine))


def solution(mesh):
    return jax.shard_map(
        shards,
        mesh=mesh,
        in_specs=(P(("dp", "tensor"), None), P(None, "dp", "tensor"), P("dp", "tensor")),
        out_specs=(P(("dp", "tensor"), None), P(None, "dp", "tensor")),
        check_vma=False,
    )
```

time: 488 us -> 142 us (0.29)
  waiting for transfers between devices: 401 us -> 0 us
  Pallas kernels: 0 us -> 139 us
  matrix products: 34.4 us -> 0 us
  local copies, waits for them, and re-layouts: 32.2 us -> 2.77 us
  between operations: 14 us -> 0.65 us
  other arithmetic: 5.26 us -> 0 us
    all_gather x2 -> x0, waiting for transfers between devices: 190 us -> none  [the longest x1 112 us: shards(): full_x = lax.all_gather(inputs, 'tensor', axis=0, tiled=True)]
    pallas_call x0 -> x1, Pallas kernels: none -> 139 us  [shards(): pl.pallas_call(kernel, out_shape=(jax.ShapeDtypeStruct((80, D), BF16), ja...]
    reduce_scatter x1 -> x0, waiting for transfers between devices: 113 us -> none  [shards(): lax.psum_scatter(x_partial.astype(jnp.bfloat16), 'tensor', scatter_dimens...]
    unnamed x5 -> x0, waiting for transfers between devices: 98.5 us -> none
    dot_general x8 -> x0, matrix products: 31.4 us -> none  [the longest x1 9.71 us: shards(): jnp.einsum('sd,jsh->jdh', full_x, grads, preferred_element_type=f32)]
    unnamed x31 -> x4, local copies, waits for them, and re-layouts: 29.6 us -> 2.77 us
  transfers between devices with their start and end apart: 4 -> 0, of which waited for: 4 -> 0; matrix products, arithmetic and copies ran while one was open for 4% -> 0% of each run, Pallas kernels for 0% -> 0%
where the time goes in v1:
time: 142 us
  Pallas kernels  139 us (98%)
  local copies, waits for them, and re-layouts  2.77 us (2%)
    pallas_call x1, Pallas kernels, shards(): pl.pallas_call(kernel, out_shape=(jax.ShapeDtypeStruct((80, D), BF16), ja...  139 us

profile of v1, /device:TPU:1, one launch (start us, length us, event | category | flops | bytes accessed | tf_op | source)
XLA Modules:
  0.0 142.3 jit_solution(10091735255866475518)
XLA Ops:
  0.6 138.9 %mixer_backward.1 = (bf16[80,4096]{1,0:T(8,128)(2,1)}, f32[3,128,256]{2,1,0:T(8,128)}) custom-call(bf16[80,4096]{1,0:T(8,128)(2,1)} %x_in.1, bf16[3,128,256]{2,1,0:T(8,128)(2,1)} %w_in.1, bf16[640,256]{1,0:T(8,128)(2,1)} %up_in.1, f32[640,128]{1,0:T(8,128)} %constant.4.clone.cos_in, f32[640,128]{1,0:T(8,128)} %constant.5.clone.sin_in), custom_call_target="tpu_custom_call" | custom-call | tf_op jit(solution)/shard_map/mixer_backward/pallas_call | solution.py:406
  139.6 0.0 copy-start
  139.6 2.0 %copy.9 = bf16[80,4096]{1,0:T(8,128)(2,1)} copy(bf16[80,4096]{1,0:T(8,128)(2,1)} %get-tuple-element.4) | data formatting | bytes 1310720
  141.6 0.0 copy-done
  141.6 0.7 copy.10
Async XLA Ops:
  139.6 2.0 %copy-start = (f32[3,128,256]{2,1,0:T(8,128)S(1)}, f32[3,128,256]{2,1,0:T(8,128)}, u32[]{:S(2)}) copy-start(f32[3,128,256]{2,1,0:T(8,128)} %get-tuple-element.5) | copy-start | bytes 1179652

commit v2 on v1

v2 whole, which is shorter than its diff:
```python
import functools

import jax
import jax.numpy as jnp
import numpy as np
from jax import lax
from jax.experimental import pallas as pl
from jax.experimental.pallas import tpu as pltpu
from jax.sharding import PartitionSpec as P

HS = 128
SEQ = 640
D = 4096
MESH = pl.DeviceIdType.MESH
F32 = jnp.float32
BF16 = jnp.bfloat16
HALF = D // 2
POSITION = {2: 0, 1: 1, -1: 2, 0: 3}


def rotary_tables():
    half = HS // 2
    frequency = 10000.0 ** (-np.arange(half, dtype=np.float64) / half)
    angles = np.arange(SEQ, dtype=np.float64)[:, None] * frequency[None, :]
    cosine, sine = np.cos(angles), np.sin(angles)
    return (
        np.concatenate([cosine, cosine], -1).astype(np.float32),
        np.concatenate([-sine, sine], -1).astype(np.float32),
    )


def dot_nn(a, b):
    return lax.dot_general(a, b, (((1,), (0,)), ((), ())), preferred_element_type=F32)


def dot_nt(a, b):
    return lax.dot_general(a, b, (((1,), (1,)), ((), ())), preferred_element_type=F32)


def dot_tn(a, b):
    return lax.dot_general(a, b, (((0,), (0,)), ((), ())), preferred_element_type=F32)


N_SEND = 96
N_RECV = 96


def kernel(
    x_in, w_in, up_in, cos_in, sin_in, dx_out, dw_out,
    xv, wv, upv, cosv, sinv, pacc, qkv, gv, gr, accv, dxp, dwp,
    rel_v, fin_v, zl_v, sib_v, xrel_v, xfin_v, zrel_v, zfin_v,
    send_sem, recv_sem, local_sem,
):
    dp = lax.axis_index("dp")
    tensor = lax.axis_index("tensor")
    x, zh, c = dp // 8, (dp // 2) % 4, dp % 2
    y, zl = tensor // 2, tensor % 2

    def place(xx, zz, cc, yy, ll):
        return {"dp": xx * 8 + zz * 2 + cc, "tensor": yy * 2 + ll}

    def ring(v, step):
        return lax.rem(v + (step + 4), 4)

    yp, ym = place(x, zh, c, ring(y, 1), zl), place(x, zh, c, ring(y, -1), zl)
    xp, xm = place(ring(x, 1), zh, c, y, zl), place(ring(x, -1), zh, c, y, zl)
    zp, zm = place(x, ring(zh, 1), c, y, zl), place(x, ring(zh, -1), c, y, zl)
    mate = place(x, zh, c, y, 1 - zl)
    sibling = place(x, zh, 1 - c, y, zl)
    everyone = (yp, ym, xp, xm, zp, zm, mate, sibling)

    keys = {}
    sends = []

    def key_index(key):
        return keys.setdefault(key, len(keys))

    def send(src, dst, key, device):
        copy = pltpu.make_async_remote_copy(
            src_ref=src, dst_ref=dst, send_sem=send_sem.at[len(sends)],
            recv_sem=recv_sem.at[key_index(key)], device_id=device, device_id_type=MESH,
        )
        copy.start()
        sends.append(copy)

    def recv(dst, key, device):
        pltpu.make_async_remote_copy(
            src_ref=dst, dst_ref=dst, send_sem=send_sem.at[0],
            recv_sem=recv_sem.at[key_index(key)], device_id=device, device_id_type=MESH,
        ).wait_recv()

    def rows(yy, ll):
        return pl.ds(pl.multiple_of(yy * 160 + ll * 80, 16), 80)

    def cols(h):
        return pl.ds(h * HALF, HALF)

    def slot(dy, dz):
        return pl.ds(160 * POSITION[dy] + 80 * dz, 80)

    own_x = xv.at[slot(0, 0)]

    def unit(xx, zz):
        return wv.at[:, xx * 4 + zz, c]

    locals_ = [
        pltpu.make_async_copy(x_in, own_x, local_sem.at[0]),
        pltpu.make_async_copy(w_in, unit(x, zh), local_sem.at[1]),
        pltpu.make_async_copy(up_in, upv, local_sem.at[2]),
        pltpu.make_async_copy(cos_in, cosv, local_sem.at[3]),
        pltpu.make_async_copy(sin_in, sinv, local_sem.at[4]),
    ]
    for copy in locals_:
        copy.start()

    barrier = pltpu.get_barrier_semaphore()
    for device in everyone:
        pl.semaphore_signal(barrier, inc=1, device_id=device, device_id_type=MESH)
    pl.semaphore_wait(barrier, len(everyone))

    top, bottom = pl.ds(0, 64), pl.ds(64, 64)

    def unit_half(xx, zz, part):
        return wv.at[:, xx * 4 + zz, c, part]

    def group(xx, cc):
        return wv.at[:, pl.ds(xx * 4, 4), cc]

    xn, xq, x2 = ring(x, -1), ring(x, 1), ring(x, 2)
    zn, zq, z2 = ring(zh, -1), ring(zh, 1), ring(zh, 2)

    def quarter(k):
        return pl.ds(k * 1024, 1024)

    def xpiece(dy, dz, part):
        return xv.at[slot(dy, dz), part]

    def to_mate(k):
        send(x_in.at[:, quarter(k)], xpiece(0, 1, quarter(k)), ("Xp", k), mate)

    to_mate(0)
    to_mate(2)
    send(w_in, unit(x, zh), ("W", 0, -1), zp)
    send(w_in, unit(x, zh), ("W", 0, 1), zm)
    for h in range(2):
        send(x_in.at[:, cols(h)], xpiece(-1, 0, cols(h)), ("Xo", -1, h), yp)
        send(x_in.at[:, cols(1 - h)], xpiece(1, 0, cols(1 - h)), ("Xo", 1, 1 - h), ym)
    send(w_in, unit(x, zh), ("W", -1, 0), xp)
    send(w_in, unit(x, zh), ("W", 1, 0), xm)
    for copy in locals_:
        copy.wait()

    def pass_on(piece, key, device):
        send(piece, piece, key, device)

    def mate_piece(k):
        piece = xpiece(0, 1, quarter(k))
        recv(piece, ("Xp", k), mate)
        send(piece, xpiece(-1, 1, quarter(k)), ("Xq", -1, k), yp)
        send(piece, xpiece(1, 1, quarter(k)), ("Xq", 1, k), ym)

    def far_piece(k):
        dy, source, device = (-1, ym, yp) if k < 2 else (1, yp, ym)
        piece = xpiece(dy, 1, quarter(k))
        recv(piece, ("Xq", dy, k), source)
        send(piece, xpiece(2, 1, quarter(k)), ("Xr", 1, k), device)

    recv(unit(xn, zh), ("W", -1, 0), xm)
    pass_on(unit(xn, zh), ("W", 2, 0), xp)
    recv(unit(xq, zh), ("W", 1, 0), xp)

    mate_piece(0)
    mate_piece(2)
    to_mate(1)
    to_mate(3)
    recv(unit(x, zn), ("W", 0, -1), zm)
    pass_on(unit_half(x, zn, top), "WrA", zp)
    pass_on(unit(x, zn), ("W", -1, -1), xp)
    pass_on(unit(x, zn), ("W", 1, -1), xm)
    recv(unit(x, zq), ("W", 0, 1), zp)
    pass_on(unit_half(x, zq, bottom), "WrB", zm)
    pass_on(unit(x, zq), ("W", -1, 1), xp)
    pass_on(unit(x, zq), ("W", 1, 1), xm)

    recv(xpiece(-1, 0, cols(0)), ("Xo", -1, 0), ym)
    send(xpiece(-1, 0, cols(0)), xpiece(2, 0, cols(0)), ("Xr", 0, 0), yp)
    recv(xpiece(1, 0, cols(1)), ("Xo", 1, 1), yp)
    send(xpiece(1, 0, cols(1)), xpiece(2, 0, cols(1)), ("Xr", 0, 1), ym)

    recv(unit_half(x, z2, top), "WrA", zm)
    recv(unit_half(x, z2, bottom), "WrB", zp)
    pass_on(unit(x, z2), ("W", -1, 2), xp)
    pass_on(unit(x, z2), ("W", 1, 2), xm)
    pass_on(group(x, c), ("S", 0), sibling)
    mate_piece(1)
    mate_piece(3)

    recv(unit(xn, zn), ("W", -1, -1), xm)
    pass_on(unit(xn, zn), ("W", 2, -1), xp)
    recv(unit(xq, zq), ("W", 1, 1), xp)
    pass_on(unit(xq, zq), ("W", 2, 1), xm)
    far_piece(0)
    far_piece(2)
    recv(unit(xq, zn), ("W", 1, -1), xp)
    recv(unit(xn, zq), ("W", -1, 1), xm)
    recv(unit(xq, z2), ("W", 1, 2), xp)
    pass_on(unit(xq, z2), ("W", 2, 2), xm)
    recv(unit(xn, z2), ("W", -1, 2), xm)
    pass_on(group(xn, c), ("S", -1), sibling)
    pass_on(group(xq, c), ("S", 1), sibling)
    far_piece(1)
    far_piece(3)

    recv(xpiece(-1, 0, cols(1)), ("Xo", -1, 1), ym)
    recv(xpiece(1, 0, cols(0)), ("Xo", 1, 0), yp)
    for k in (2, 3):
        recv(xpiece(-1, 1, quarter(k)), ("Xq", -1, k), ym)
    for k in (0, 1):
        recv(xpiece(1, 1, quarter(k)), ("Xq", 1, k), yp)
    near_rows = pl.ds(160, 480)

    def project_group(xx, first):
        @pl.loop(0, 3)
        def _(j):
            t = dot_nn(
                xv[near_rows, pl.ds(pl.multiple_of(xx * 1024, 1024), 1024)],
                wv[j, pl.ds(xx * 4, 4)].reshape(1024, 256),
            )
            if first:
                pacc[j, near_rows] = t
            else:
                pacc[j, near_rows] += t

    recv(group(x, 1 - c), ("S", 0), sibling)
    project_group(x, True)
    recv(group(xn, 1 - c), ("S", -1), sibling)
    project_group(xn, False)
    recv(unit(x2, zh), ("W", 2, 0), xm)
    recv(unit(x2, zn), ("W", 2, -1), xm)
    recv(unit(x2, zq), ("W", 2, 1), xp)
    recv(unit(x2, z2), ("W", 2, 2), xp)
    pass_on(group(x2, c), ("S", 2), sibling)
    recv(group(xq, 1 - c), ("S", 1), sibling)
    project_group(xq, False)
    recv(group(x2, 1 - c), ("S", 2), sibling)
    project_group(x2, False)

    def place_rows(j, dy, dz, p):
        r = rows(ring(y, dy), zl if dz == 0 else 1 - zl)
        rotated = j < 2
        cc = jnp.where(rotated, cosv[r], 1.0)
        ss = jnp.where(rotated, sinv[r], 0.0)
        for h in range(2):
            ph = p[:, h * HS:(h + 1) * HS]
            qkv[j, h, r] = (ph * cc + pltpu.roll(ph, 64, 1) * ss).astype(BF16)

    @pl.loop(0, 3)
    def _(j):
        for dy in (1, -1, 0):
            for dz in range(2):
                place_rows(j, dy, dz, pacc[j, slot(dy, dz)])

    recv(xpiece(2, 0, cols(0)), ("Xr", 0, 0), ym)
    recv(xpiece(2, 0, cols(1)), ("Xr", 0, 1), yp)
    for k in (0, 1):
        recv(xpiece(2, 1, quarter(k)), ("Xr", 1, k), ym)
    for k in (2, 3):
        recv(xpiece(2, 1, quarter(k)), ("Xr", 1, k), yp)

    @pl.loop(0, 3)
    def _(j):
        p = dot_nn(xv[pl.ds(0, 160)], wv[j].reshape(D, 256))
        for dz in range(2):
            place_rows(j, 2, dz, p[dz * 80:(dz + 1) * 80])

    scale = HS ** -0.5
    lower = lax.broadcasted_iota(jnp.int32, (128, 128), 0) >= lax.broadcasted_iota(
        jnp.int32, (128, 128), 1
    )

    def rotate_back(v, r):
        return (v * cosv[r] - pltpu.roll(v, 64, 1) * sinv[r]).astype(BF16)

    heads = range(2)
    for i in reversed(range(5)):
        n = (i + 1) * 128
        r, head = pl.ds(i * 128, 128), pl.ds(0, n)
        q = [qkv[0, h, r] for h in heads]
        k = [qkv[1, h, head] for h in heads]
        v = [qkv[2, h, head] for h in heads]
        up = [upv[r, pl.ds(h * HS, HS)] for h in heads]
        s = [dot_nt(q[h], k[h]) for h in heads]
        gp = [dot_nt(up[h], v[h]) for h in heads]
        low, gs = [], []
        for h in heads:
            diagonal = jnp.where(lower, s[h][:, i * 128:], -1e30)
            if i:
                diagonal = jnp.concatenate([s[h][:, : i * 128], diagonal], 1)
            top_score = jnp.max(diagonal, 1, keepdims=True)
            e = jnp.exp2((diagonal - top_score) * (scale * np.log2(np.e)))
            prob = e * (1.0 / jnp.sum(e, 1, keepdims=True))
            low.append(prob.astype(BF16))
            dots = jnp.sum(low[h].astype(F32) * gp[h], 1, keepdims=True)
            gs.append((prob * (gp[h] - dots)).astype(BF16))
        for h in heads:
            gv[r, pl.ds(h * HS, HS)] = rotate_back(dot_nn(gs[h], k[h]) * scale, r)
            dk, dv = dot_tn(gs[h], q[h]), dot_tn(low[h], up[h])
            if i == 4:
                accv[h], accv[2 + h] = dk, dv
            else:
                accv[h, head] += dk
                accv[2 + h, head] += dv
    full = pl.ds(0, SEQ)
    for h in heads:
        gv[:, pl.ds(256 + h * HS, HS)] = rotate_back(accv[h] * scale, full)
        gv[:, pl.ds(512 + h * HS, HS)] = accv[2 + h].astype(BF16)
    for dy in POSITION:
        for dz in range(2):
            gr[slot(dy, dz)] = gv[rows(ring(y, dy), zl if dz == 0 else 1 - zl)]

    def x_term(first, count):
        r = pl.ds(first, count)

        @pl.loop(0, 4)
        def _(i):
            total = None
            for j in range(3):
                w = wv[j, pl.ds(i * 4, 4)].reshape(1024, 256)
                t = dot_nt(gr[r, pl.ds(j * 256, 256)], w)
                total = t if total is None else total + t
            dxp[r, pl.ds(pl.multiple_of(i * 1024, 1024), 1024)] = total.astype(BF16)

    def w_term(xx):
        @pl.loop(0, 4)
        def _(i):
            b = xx * 4 + i
            t = dot_tn(xv[:, pl.ds(pl.multiple_of(b * 256, 256), 256)], gr[...])
            for cc in range(2):
                for j in range(3):
                    dwp[b, cc, j] = t[cc * 128:(cc + 1) * 128, j * 256:(j + 1) * 256].astype(BF16)

    def add_into(dst, src):
        dst[...] = (dst[...].astype(F32) + src[...].astype(F32)).astype(BF16)

    def add_two(dst, one, two):
        dst[...] = (
            dst[...].astype(F32) + one[...].astype(F32) + two[...].astype(F32)
        ).astype(BF16)

    def xpart(dy, dz, part):
        return dxp.at[slot(dy, dz), part]

    def wunit(xx, zz):
        return dwp.at[xx * 4 + zz, c]

    def send_sib(xx, dx):
        send(dwp.at[pl.ds(xx * 4, 4), 1 - c], sib_v.at[pl.ds(xx * 4, 4)], ("DS", dx), sibling)

    def recv_sib(xx, dx):
        recv(sib_v.at[pl.ds(xx * 4, 4)], ("DS", dx), sibling)

        @pl.loop(0, 4)
        def _(i):
            add_into(dwp.at[xx * 4 + i, c], sib_v.at[xx * 4 + i])

    def far_x(dz):
        send(xpart(2, dz, cols(0)), rel_v.at[0, dz], ("R", 0, dz), yp)
        send(xpart(2, dz, cols(1)), rel_v.at[1, dz], ("R", 1, dz), ym)

    def near_x(s, dz, h):
        dy, device = ((1, yp), (-1, ym))[s]
        send(xpart(dy, dz, cols(h)), fin_v.at[s, dz, h], ("F", s, dz, h), device)

    def relay_x(dz):
        recv(rel_v.at[0, dz], ("R", 0, dz), ym)
        add_into(xpart(1, dz, cols(0)), rel_v.at[0, dz])
        near_x(0, dz, 0)
        recv(rel_v.at[1, dz], ("R", 1, dz), yp)
        add_into(xpart(-1, dz, cols(1)), rel_v.at[1, dz])
        near_x(1, dz, 1)

    def recv_near(s, dz, h):
        recv(fin_v.at[s, dz, h], ("F", s, dz, h), (ym, yp)[s])

    up_units, down_units = (2, -1), (1, 0)
    zs = {0: zh, 1: zq, 2: z2, -1: zn}

    def far_w(dz):
        if dz in up_units:
            send(wunit(x2, zs[dz]), xrel_v.at[zs[dz]], ("XR", dz), xp)
        else:
            send(wunit(x2, zs[dz]), xrel_v.at[zs[dz]], ("XR", dz), xm)

    def relay_w(dz):
        if dz in up_units:
            recv(xrel_v.at[zs[dz]], ("XR", dz), xm)
            add_into(wunit(xq, zs[dz]), xrel_v.at[zs[dz]])
        else:
            recv(xrel_v.at[zs[dz]], ("XR", dz), xp)
            add_into(wunit(xn, zs[dz]), xrel_v.at[zs[dz]])

    def near_w(dz):
        relay_w(dz)
        send(wunit(xq, zs[dz]), xfin_v.at[0, zs[dz]], ("XF", 0, dz), xp)
        send(wunit(xn, zs[dz]), xfin_v.at[1, zs[dz]], ("XF", 1, dz), xm)

    def sum_w(dz):
        recv(xfin_v.at[0, zs[dz]], ("XF", 0, dz), xm)
        recv(xfin_v.at[1, zs[dz]], ("XF", 1, dz), xp)
        add_two(wunit(x, zs[dz]), xfin_v.at[0, zs[dz]], xfin_v.at[1, zs[dz]])

    def wz_half(zz, part):
        return dwp.at[x * 4 + zz, c, :, part]

    def mate_x(h):
        add_two(xpart(0, 1, cols(h)), fin_v.at[0, 1, h], fin_v.at[1, 1, h])
        send(xpart(0, 1, cols(h)), zl_v.at[h], ("Z", h), mate)

    x_term(0, 160)
    far_x(1)
    w_term(x2)
    send_sib(x2, 2)
    x_term(160, 480)
    near_x(0, 1, 1)
    near_x(1, 1, 0)
    recv_sib(x2, 2)
    far_w(2)
    far_w(1)
    w_term(xq)
    send_sib(xq, 1)
    w_term(xn)
    send_sib(xn, -1)
    relay_x(1)
    recv_sib(xq, 1)
    recv_sib(xn, -1)
    near_w(2)
    w_term(x)
    send_sib(x, 0)
    near_w(1)
    far_w(-1)
    far_w(0)
    recv_near(0, 1, 1)
    recv_near(1, 1, 0)
    far_x(0)
    recv_sib(x, 0)
    sum_w(2)
    send(wz_half(z2, top), zrel_v.at[0], ("ZR", 0), zp)
    send(wz_half(z2, bottom), zrel_v.at[1], ("ZR", 1), zm)
    recv_near(0, 1, 0)
    mate_x(0)
    recv_near(1, 1, 1)
    mate_x(1)
    near_x(0, 0, 1)
    near_x(1, 0, 0)
    near_w(-1)
    sum_w(1)
    send(wz_half(zq, bottom), zfin_v.at[0, :, bottom], ("ZF", 0, 1), zp)
    near_w(0)
    sum_w(-1)
    send(wz_half(zn, top), zfin_v.at[1, :, top], ("ZF", 1, 0), zm)
    recv(zrel_v.at[0], ("ZR", 0), zm)
    add_into(wz_half(zq, top), zrel_v.at[0])
    send(wz_half(zq, top), zfin_v.at[0, :, top], ("ZF", 0, 0), zp)
    recv(zrel_v.at[1], ("ZR", 1), zp)
    add_into(wz_half(zn, bottom), zrel_v.at[1])
    send(wz_half(zn, bottom), zfin_v.at[1, :, bottom], ("ZF", 1, 1), zm)
    relay_x(0)
    sum_w(0)

    recv(zfin_v.at[0, :, bottom], ("ZF", 0, 1), zm)
    recv(zfin_v.at[0, :, top], ("ZF", 0, 0), zm)
    recv(zfin_v.at[1, :, top], ("ZF", 1, 0), zp)
    recv(zfin_v.at[1, :, bottom], ("ZF", 1, 1), zp)
    dw_out[...] = (
        wunit(x, zh)[...].astype(F32) + zfin_v[0].astype(F32) + zfin_v[1].astype(F32)
    )

    for h in range(2):
        recv(zl_v.at[h], ("Z", h), mate)
        recv_near(0, 0, h)
        recv_near(1, 0, h)
        dx_out[:, h * HALF:(h + 1) * HALF] = (
            xpart(0, 0, cols(h))[...].astype(F32)
            + fin_v[0, 0, h].astype(F32)
            + fin_v[1, 0, h].astype(F32)
            + zl_v[h].astype(F32)
        ).astype(BF16)

    for copy in sends:
        copy.wait_send()
    assert len(sends) <= N_SEND and len(keys) <= N_RECV


def shards(inputs, projections, upstream_grad):
    cosine, sine = rotary_tables()
    any_spec = pl.BlockSpec(memory_space=pl.ANY)
    vmem = pl.BlockSpec(memory_space=pltpu.VMEM)
    return pl.pallas_call(
        kernel,
        out_shape=(
            jax.ShapeDtypeStruct((80, D), BF16),
            jax.ShapeDtypeStruct((3, 128, 256), F32),
        ),
        in_specs=[any_spec] * 5,
        out_specs=(vmem, vmem),
        scratch_shapes=[
            pltpu.VMEM((SEQ, D), BF16),
            pltpu.VMEM((3, 16, 2, 128, 256), BF16),
            pltpu.VMEM((SEQ, 256), BF16),
            pltpu.VMEM((SEQ, HS), F32),
            pltpu.VMEM((SEQ, HS), F32),
            pltpu.VMEM((3, SEQ, 256), F32),
            pltpu.VMEM((3, 2, SEQ, HS), BF16),
            pltpu.VMEM((SEQ, 768), BF16),
            pltpu.VMEM((SEQ, 768), BF16),
            pltpu.VMEM((4, SEQ, HS), F32),
            pltpu.VMEM((SEQ, D), BF16),
            pltpu.VMEM((16, 2, 3, 128, 256), BF16),
            pltpu.VMEM((2, 2, 80, HALF), BF16),
            pltpu.VMEM((2, 2, 2, 80, HALF), BF16),
            pltpu.VMEM((2, 80, HALF), BF16),
            pltpu.VMEM((16, 3, 128, 256), BF16),
            pltpu.VMEM((4, 3, 128, 256), BF16),
            pltpu.VMEM((2, 4, 3, 128, 256), BF16),
            pltpu.VMEM((2, 3, 64, 256), BF16),
            pltpu.VMEM((2, 3, 128, 256), BF16),
            pltpu.SemaphoreType.DMA((N_SEND,)),
            pltpu.SemaphoreType.DMA((N_RECV,)),
            pltpu.SemaphoreType.DMA((5,)),
        ],
        compiler_params=pltpu.CompilerParams(
            collective_id=0, has_side_effects=True, vmem_limit_bytes=60 * 2**20
        ),
        name="mixer_backward",
    )(inputs, projections, upstream_grad, jnp.asarray(cosine), jnp.asarray(sine))


def solution(mesh):
    return jax.shard_map(
        shards,
        mesh=mesh,
        in_specs=(P(("dp", "tensor"), None), P(None, "dp", "tensor"), P("dp", "tensor")),
        out_specs=(P(("dp", "tensor"), None), P(None, "dp", "tensor")),
        check_vma=False,
    )
```

time: 142 us -> 120 us (0.85)
  Pallas kernels: 139 us -> 116 us
    pallas_call x1, Pallas kernels: 139 us -> 116 us  [shards(): pl.pallas_call(kernel, out_shape=(jax.ShapeDtypeStruct((80, D), BF16), ja...]
where the time goes in v2:
time: 120 us
  Pallas kernels  116 us (97%)
  local copies, waits for them, and re-layouts  2.77 us (2%)
    pallas_call x1, Pallas kernels, shards(): pl.pallas_call(kernel, out_shape=(jax.ShapeDtypeStruct((80, D), BF16), ja...  116 us
    unnamed x4, local copies, waits for them, and re-layouts  2.77 us

profile of v2, /device:TPU:1, one launch (start us, length us, event | category | flops | bytes accessed | tf_op | source)
XLA Modules:
  0.0 119.6 jit_solution(3091357579350394206)
XLA Ops:
  0.6 116.2 %mixer_backward.1 = (bf16[80,4096]{1,0:T(8,128)(2,1)}, f32[3,128,256]{2,1,0:T(8,128)}) custom-call(bf16[80,4096]{1,0:T(8,128)(2,1)} %x_in.1, bf16[3,128,256]{2,1,0:T(8,128)(2,1)} %w_in.1, bf16[640,256]{1,0:T(8,128)(2,1)} %up_in.1, f32[640,128]{1,0:T(8,128)} %constant.4.clone.cos_in, f32[640,128]{1,0:T(8,128)} %constant.5.clone.sin_in), custom_call_target="tpu_custom_call" | custom-call | tf_op jit(solution)/shard_map/mixer_backward/pallas_call | solution.py:498
  116.8 0.0 copy-start
  116.8 2.0 %copy.9 = bf16[80,4096]{1,0:T(8,128)(2,1)} copy(bf16[80,4096]{1,0:T(8,128)(2,1)} %get-tuple-element.4) | data formatting | bytes 1310720
  118.8 0.0 copy-done
  118.8 0.7 copy.10
Async XLA Ops:
  116.8 2.0 %copy-start = (f32[3,128,256]{2,1,0:T(8,128)S(1)}, f32[3,128,256]{2,1,0:T(8,128)}, u32[]{:S(2)}) copy-start(f32[3,128,256]{2,1,0:T(8,128)} %get-tuple-element.5) | copy-start | bytes 1179652

commit v3 on v2

--- a/solution.py
+++ b/solution.py
@@ -15,6 +15,7 @@
 F32 = jnp.float32
 BF16 = jnp.bfloat16
 HALF = D // 2
+MIDDLE = pl.ds(1536, 1024)
 POSITION = {2: 0, 1: 1, -1: 2, 0: 3}
 
 
@@ -48,7 +49,7 @@
 def kernel(
     x_in, w_in, up_in, cos_in, sin_in, dx_out, dw_out,
     xv, wv, upv, cosv, sinv, pacc, qkv, gv, gr, accv, dxp, dwp,
-    rel_v, fin_v, zl_v, sib_v, xrel_v, xfin_v, zrel_v, zfin_v,
+    rel_v, fin_v, zl_v, zb_v, sib_v, xrel_v, xfin_v, zrel_v, zfin_v,
     send_sem, recv_sem, local_sem,
 ):
     dp = lax.axis_index("dp")
@@ -130,7 +131,7 @@
     zn, zq, z2 = ring(zh, -1), ring(zh, 1), ring(zh, 2)
 
     def quarter(k):
-        return pl.ds(k * 1024, 1024)
+        return pl.ds((0, 768, 2560, 3328)[k], 768)
 
     def xpiece(dy, dz, part):
         return xv.at[slot(dy, dz), part]
@@ -187,6 +188,10 @@
     recv(xpiece(1, 0, cols(1)), ("Xo", 1, 1), yp)
     send(xpiece(1, 0, cols(1)), xpiece(2, 0, cols(1)), ("Xr", 0, 1), ym)
 
+    def middle_piece(dy):
+        send(xpiece(dy, 0, MIDDLE), xpiece(dy, 1, MIDDLE), ("Xb", dy), mate)
+
+
     recv(unit_half(x, z2, top), "WrA", zm)
     recv(unit_half(x, z2, bottom), "WrB", zp)
     pass_on(unit(x, z2), ("W", -1, 2), xp)
@@ -194,6 +199,11 @@
     pass_on(group(x, c), ("S", 0), sibling)
     mate_piece(1)
     mate_piece(3)
+    middle_piece(0)
+    recv(xpiece(-1, 0, cols(1)), ("Xo", -1, 1), ym)
+    middle_piece(-1)
+    recv(xpiece(1, 0, cols(0)), ("Xo", 1, 0), yp)
+    middle_piece(1)
 
     recv(unit(xn, zn), ("W", -1, -1), xm)
     pass_on(unit(xn, zn), ("W", 2, -1), xp)
@@ -211,8 +221,11 @@
     far_piece(1)
     far_piece(3)
 
-    recv(xpiece(-1, 0, cols(1)), ("Xo", -1, 1), ym)
-    recv(xpiece(1, 0, cols(0)), ("Xo", 1, 0), yp)
+    recv(xpiece(2, 0, cols(0)), ("Xr", 0, 0), ym)
+    recv(xpiece(2, 0, cols(1)), ("Xr", 0, 1), yp)
+    middle_piece(2)
+    for dy in (0, -1, 1):
+        recv(xpiece(dy, 1, MIDDLE), ("Xb", dy), mate)
     for k in (2, 3):
         recv(xpiece(-1, 1, quarter(k)), ("Xq", -1, k), ym)
     for k in (0, 1):
@@ -260,8 +273,7 @@
             for dz in range(2):
                 place_rows(j, dy, dz, pacc[j, slot(dy, dz)])
 
-    recv(xpiece(2, 0, cols(0)), ("Xr", 0, 0), ym)
-    recv(xpiece(2, 0, cols(1)), ("Xr", 0, 1), yp)
+    recv(xpiece(2, 1, MIDDLE), ("Xb", 2), mate)
     for k in (0, 1):
         recv(xpiece(2, 1, quarter(k)), ("Xr", 1, k), ym)
     for k in (2, 3):
@@ -318,17 +330,14 @@
         for dz in range(2):
             gr[slot(dy, dz)] = gv[rows(ring(y, dy), zl if dz == 0 else 1 - zl)]
 
-    def x_term(first, count):
-        r = pl.ds(first, count)
-
-        @pl.loop(0, 4)
-        def _(i):
-            total = None
-            for j in range(3):
-                w = wv[j, pl.ds(i * 4, 4)].reshape(1024, 256)
-                t = dot_nt(gr[r, pl.ds(j * 256, 256)], w)
-                total = t if total is None else total + t
-            dxp[r, pl.ds(pl.multiple_of(i * 1024, 1024), 1024)] = total.astype(BF16)
+    def x_term(first, count, part):
+        r, depth = pl.ds(first, count), part.size
+        total = None
+        for j in range(3):
+            w = wv[j, pl.ds(part.start // 256, depth // 256)].reshape(depth, 256)
+            t = dot_nt(gr[r, pl.ds(j * 256, 256)], w)
+            total = t if total is None else total + t
+        dxp[r, part] = total.astype(BF16)
 
     def w_term(xx):
         @pl.loop(0, 4)
@@ -363,24 +372,43 @@
         def _(i):
             add_into(dwp.at[xx * 4 + i, c], sib_v.at[xx * 4 + i])
 
-    def far_x(dz):
-        send(xpart(2, dz, cols(0)), rel_v.at[0, dz], ("R", 0, dz), yp)
-        send(xpart(2, dz, cols(1)), rel_v.at[1, dz], ("R", 1, dz), ym)
+    def side(h, dz):
+        if dz == 0:
+            return cols(h)
+        return pl.ds((0, 2560)[h], 1536)
+
+    def kept(dz):
+        return pl.ds(0, HALF if dz == 0 else 1536)
+
+    def far_x(h, p):
+        send(
+            xpart(2, 1, quarter(2 * h + p)), rel_v.at[h, 1, :, pl.ds(768 * p, 768)],
+            ("R", h, 1, p), (yp, ym)[h],
+        )
 
     def near_x(s, dz, h):
         dy, device = ((1, yp), (-1, ym))[s]
-        send(xpart(dy, dz, cols(h)), fin_v.at[s, dz, h], ("F", s, dz, h), device)
+        send(xpart(dy, dz, side(h, dz)), fin_v.at[s, dz, h, :, kept(dz)], ("F", s, dz, h), device)
 
     def relay_x(dz):
-        recv(rel_v.at[0, dz], ("R", 0, dz), ym)
-        add_into(xpart(1, dz, cols(0)), rel_v.at[0, dz])
-        near_x(0, dz, 0)
-        recv(rel_v.at[1, dz], ("R", 1, dz), yp)
-        add_into(xpart(-1, dz, cols(1)), rel_v.at[1, dz])
-        near_x(1, dz, 1)
+        for h, dy, source in ((0, 1, ym), (1, -1, yp)):
+            if dz == 0:
+                recv(rel_v.at[h, 0], ("R", h, 0), source)
+            else:
+                for p in range(2):
+                    recv(rel_v.at[h, 1, :, pl.ds(768 * p, 768)], ("R", h, 1, p), source)
+            add_into(xpart(dy, dz, side(h, dz)), rel_v.at[h, dz, :, kept(dz)])
+            near_x(h, dz, h)
+
+    def middle_x(dy):
+        send(xpart(dy, 1, MIDDLE), zb_v.at[POSITION[dy]], ("ZB", dy), mate)
+
+    def add_middle(dy):
+        recv(zb_v.at[POSITION[dy]], ("ZB", dy), mate)
+        add_into(xpart(dy, 0, MIDDLE), zb_v.at[POSITION[dy]])
 
     def recv_near(s, dz, h):
-        recv(fin_v.at[s, dz, h], ("F", s, dz, h), (ym, yp)[s])
+        recv(fin_v.at[s, dz, h, :, kept(dz)], ("F", s, dz, h), (ym, yp)[s])
 
     up_units, down_units = (2, -1), (1, 0)
     zs = {0: zh, 1: zq, 2: z2, -1: zn}
@@ -413,14 +441,21 @@
         return dwp.at[x * 4 + zz, c, :, part]
 
     def mate_x(h):
-        add_two(xpart(0, 1, cols(h)), fin_v.at[0, 1, h], fin_v.at[1, 1, h])
-        send(xpart(0, 1, cols(h)), zl_v.at[h], ("Z", h), mate)
-
-    x_term(0, 160)
-    far_x(1)
+        part = xpart(0, 1, side(h, 1))
+        add_two(part, fin_v.at[0, 1, h, :, kept(1)], fin_v.at[1, 1, h, :, kept(1)])
+        send(part, zl_v.at[h], ("Z", h), mate)
+
+    for p in range(2):
+        for h in range(2):
+            x_term(0, 160, quarter(2 * h + p))
+            far_x(h, p)
+    x_term(0, SEQ, MIDDLE)
+    for dy in POSITION:
+        middle_x(dy)
     w_term(x2)
     send_sib(x2, 2)
-    x_term(160, 480)
+    for k in range(4):
+        x_term(160, 480, quarter(k))
     near_x(0, 1, 1)
     near_x(1, 1, 0)
     recv_sib(x2, 2)
@@ -441,7 +476,9 @@
     far_w(0)
     recv_near(0, 1, 1)
     recv_near(1, 1, 0)
-    far_x(0)
+    add_middle(2)
+    send(xpart(2, 0, cols(0)), rel_v.at[0, 0], ("R", 0, 0), yp)
+    send(xpart(2, 0, cols(1)), rel_v.at[1, 0], ("R", 1, 0), ym)
     recv_sib(x, 0)
     sum_w(2)
     send(wz_half(z2, top), zrel_v.at[0], ("ZR", 0), zp)
@@ -450,8 +487,11 @@
     mate_x(0)
     recv_near(1, 1, 1)
     mate_x(1)
+    add_middle(1)
+    add_middle(-1)
     near_x(0, 0, 1)
     near_x(1, 0, 0)
+    add_middle(0)
     near_w(-1)
     sum_w(1)
     send(wz_half(zq, bottom), zfin_v.at[0, :, bottom], ("ZF", 0, 1), zp)
@@ -479,12 +519,17 @@
         recv(zl_v.at[h], ("Z", h), mate)
         recv_near(0, 0, h)
         recv_near(1, 0, h)
-        dx_out[:, h * HALF:(h + 1) * HALF] = (
+        total = (
             xpart(0, 0, cols(h))[...].astype(F32)
             + fin_v[0, 0, h].astype(F32)
             + fin_v[1, 0, h].astype(F32)
-            + zl_v[h].astype(F32)
-        ).astype(BF16)
+        )
+        if h == 0:
+            dx_out[:, :1536] = (total[:, :1536] + zl_v[0].astype(F32)).astype(BF16)
+            dx_out[:, 1536:HALF] = total[:, 1536:].astype(BF16)
+        else:
+            dx_out[:, HALF:2560] = total[:, :512].astype(BF16)
+            dx_out[:, 2560:] = (total[:, 512:] + zl_v[1].astype(F32)).astype(BF16)
 
     for copy in sends:
         copy.wait_send()
@@ -518,7 +563,8 @@
             pltpu.VMEM((16, 2, 3, 128, 256), BF16),
             pltpu.VMEM((2, 2, 80, HALF), BF16),
             pltpu.VMEM((2, 2, 2, 80, HALF), BF16),
-            pltpu.VMEM((2, 80, HALF), BF16),
+            pltpu.VMEM((2, 80, 1536), BF16),
+            pltpu.VMEM((4, 80, 1024), BF16),
             pltpu.VMEM((16, 3, 128, 256), BF16),
             pltpu.VMEM((4, 3, 128, 256), BF16),
             pltpu.VMEM((2, 4, 3, 128, 256), BF16),

time: 120 us -> 113 us (0.942)
  Pallas kernels: 116 us -> 109 us
    pallas_call x1, Pallas kernels: 116 us -> 109 us  [shards(): pl.pallas_call(kernel, out_shape=(jax.ShapeDtypeStruct((80, D), BF16), ja...]
where the time goes in v3:
time: 113 us
  Pallas kernels  109 us (96%)
  local copies, waits for them, and re-layouts  2.77 us (2%)
    pallas_call x1, Pallas kernels, shards(): pl.pallas_call(kernel, out_shape=(jax.ShapeDtypeStruct((80, D), BF16), ja...  109 us
    unnamed x4, local copies, waits for them, and re-layouts  2.77 us

profile of v3, /device:TPU:1, one launch (start us, length us, event | category | flops | bytes accessed | tf_op | source)
XLA Modules:
  0.0 112.7 jit_solution(2234203974914657386)
XLA Ops:
  0.6 109.3 %mixer_backward.1 = (bf16[80,4096]{1,0:T(8,128)(2,1)}, f32[3,128,256]{2,1,0:T(8,128)}) custom-call(bf16[80,4096]{1,0:T(8,128)(2,1)} %x_in.1, bf16[3,128,256]{2,1,0:T(8,128)(2,1)} %w_in.1, bf16[640,256]{1,0:T(8,128)(2,1)} %up_in.1, f32[640,128]{1,0:T(8,128)} %constant.4.clone.cos_in, f32[640,128]{1,0:T(8,128)} %constant.5.clone.sin_in), custom_call_target="tpu_custom_call" | custom-call | tf_op jit(solution)/shard_map/mixer_backward/pallas_call | solution.py:543
  109.9 0.0 copy-start
  109.9 2.0 %copy.9 = bf16[80,4096]{1,0:T(8,128)(2,1)} copy(bf16[80,4096]{1,0:T(8,128)(2,1)} %get-tuple-element.4) | data formatting | bytes 1310720
  111.9 0.0 copy-done
  111.9 0.7 copy.10
Async XLA Ops:
  109.9 2.0 %copy-start = (f32[3,128,256]{2,1,0:T(8,128)S(1)}, f32[3,128,256]{2,1,0:T(8,128)}, u32[]{:S(2)}) copy-start(f32[3,128,256]{2,1,0:T(8,128)} %get-tuple-element.5) | copy-start | bytes 1179652

commit v4 on v3

--- a/solution.py
+++ b/solution.py
@@ -16,6 +16,10 @@
 BF16 = jnp.bfloat16
 HALF = D // 2
 MIDDLE = pl.ds(1536, 1024)
+W_PAIRS = (
+    ((2, 2), (2, 1)), ((1, 2), (-1, 2)), ((2, -1), (2, 0)), ((1, 1), (-1, 1)),
+    ((1, -1), (-1, -1)), ((0, 2), (0, 1)), ((1, 0), (-1, 0)), ((0, -1), (0, 0)),
+)
 POSITION = {2: 0, 1: 1, -1: 2, 0: 3}
 
 
@@ -42,15 +46,15 @@
     return lax.dot_general(a, b, (((0,), (0,)), ((), ())), preferred_element_type=F32)
 
 
-N_SEND = 96
-N_RECV = 96
+N_SEND = 128
+N_RECV = 128
 
 
 def kernel(
     x_in, w_in, up_in, cos_in, sin_in, dx_out, dw_out,
-    xv, wv, upv, cosv, sinv, pacc, qkv, gv, gr, accv, dxp, dwp,
+    xv, wv, upv, cosv, sinv, pacc, qkv, gv, gr, gt, accv, dxp, dwp,
     rel_v, fin_v, zl_v, zb_v, sib_v, xrel_v, xfin_v, zrel_v, zfin_v,
-    send_sem, recv_sem, local_sem,
+    send_sem, recv_sem, local_sem, far_sem, sib_sem,
 ):
     dp = lax.axis_index("dp")
     tensor = lax.axis_index("tensor")
@@ -330,31 +334,64 @@
         for dz in range(2):
             gr[slot(dy, dz)] = gv[rows(ring(y, dy), zl if dz == 0 else 1 - zl)]
 
-    def x_term(first, count, part):
-        r, depth = pl.ds(first, count), part.size
+    zs = {0: zh, 1: zq, 2: z2, -1: zn}
+
+    def x_term(i):
         total = None
         for j in range(3):
-            w = wv[j, pl.ds(part.start // 256, depth // 256)].reshape(depth, 256)
-            t = dot_nt(gr[r, pl.ds(j * 256, 256)], w)
+            w = wv[j, pl.ds(i * 2, 2)].reshape(512, 256)
+            t = dot_nt(gr[:, j * 256:(j + 1) * 256], w)
             total = t if total is None else total + t
-        dxp[r, part] = total.astype(BF16)
-
-    def w_term(xx):
-        @pl.loop(0, 4)
-        def _(i):
-            b = xx * 4 + i
-            t = dot_tn(xv[:, pl.ds(pl.multiple_of(b * 256, 256), 256)], gr[...])
+        dxp[:, pl.ds(pl.multiple_of(i * 512, 512), 512)] = total.astype(BF16)
+
+    far_key = len(keys)
+    for p in range(3):
+        for h in range(2):
+            key_index(("R", 1, p, h))
+    sibling_key = len(keys)
+    for pair in W_PAIRS:
+        for dx, dz in pair:
+            key_index(("DS", dx, dz))
+
+    def w_terms(n):
+        (dx0, dz0), (dx1, dz1) = W_PAIRS[n]
+        b0 = ring(x, dx0) * 4 + zs[dz0]
+        b1 = ring(x, dx1) * 4 + zs[dz1]
+
+        @pl.loop(0, 2)
+        def _(step):
+            b = b0 + step * (b1 - b0)
+            t = dot_nn(gt[...], xv[:, pl.ds(pl.multiple_of(b * 256, 256), 256)])
             for cc in range(2):
                 for j in range(3):
-                    dwp[b, cc, j] = t[cc * 128:(cc + 1) * 128, j * 256:(j + 1) * 256].astype(BF16)
+                    dwp[b, cc, j] = t[j * 256:(j + 1) * 256, cc * 128:(cc + 1) * 128].astype(BF16)
+            pltpu.make_async_remote_copy(
+                src_ref=dwp.at[b, 1 - c], dst_ref=sib_v.at[b],
+                send_sem=sib_sem.at[n, step], recv_sem=recv_sem.at[sibling_key + 2 * n + step],
+                device_id=sibling, device_id_type=MESH,
+            ).start()
+
+    def w_sibling(dx, dz):
+        b = ring(x, dx) * 4 + zs[dz]
+        recv(sib_v.at[b], ("DS", dx, dz), sibling)
+        add_into(dwp.at[b, c], sib_v.at[b])
+
+    def add_rows(dst, *parts):
+        rows_, step = dst.shape[0], 16 if len(dst.shape) == 2 else 1
+
+        @pl.loop(0, rows_ // step)
+        def _(i):
+            r = pl.ds(pl.multiple_of(i * step, step), step)
+            total = dst[r].astype(F32)
+            for part in parts:
+                total = total + part[r].astype(F32)
+            dst[r] = total.astype(BF16)
 
     def add_into(dst, src):
-        dst[...] = (dst[...].astype(F32) + src[...].astype(F32)).astype(BF16)
+        add_rows(dst, src)
 
     def add_two(dst, one, two):
-        dst[...] = (
-            dst[...].astype(F32) + one[...].astype(F32) + two[...].astype(F32)
-        ).astype(BF16)
+        add_rows(dst, one, two)
 
     def xpart(dy, dz, part):
         return dxp.at[slot(dy, dz), part]
@@ -362,43 +399,57 @@
     def wunit(xx, zz):
         return dwp.at[xx * 4 + zz, c]
 
-    def send_sib(xx, dx):
-        send(dwp.at[pl.ds(xx * 4, 4), 1 - c], sib_v.at[pl.ds(xx * 4, 4)], ("DS", dx), sibling)
-
-    def recv_sib(xx, dx):
-        recv(sib_v.at[pl.ds(xx * 4, 4)], ("DS", dx), sibling)
-
-        @pl.loop(0, 4)
+    def side(h, part):
+        return pl.ds((1536, 2048)[h], 512) if part == 2 else pl.ds((0, 2560)[h], 1536)
+
+    def piece(dy, part, h):
+        return xpart(dy, part % 2, side(h, part))
+
+    def arrivals(ref, part, *index):
+        return ref.at[(*index, part, slice(None), pl.ds(0, 512 if part == 2 else 1536))]
+
+    def far_own(part):
+        for h in range(2):
+            send(piece(2, part, h), arrivals(rel_v, part, h), ("R", h, part), (yp, ym)[h])
+
+    def near_x(s, part, h):
+        dy, device = ((1, yp), (-1, ym))[s]
+        send(piece(dy, part, h), arrivals(fin_v, part, s, h), ("F", s, part, h), device)
+
+    def near_both(part):
+        near_x(0, part, 1)
+        near_x(1, part, 0)
+
+    def relay_x(part, h):
+        dy, source = ((1, ym), (-1, yp))[h]
+        if part == 1:
+            for p in range(3):
+                recv(rel_v.at[h, 1, :, pl.ds(512 * p, 512)], ("R", 1, p, h), source)
+        else:
+            recv(arrivals(rel_v, part, h), ("R", h, part), source)
+        add_into(piece(dy, part, h), arrivals(rel_v, part, h))
+        near_x(h, part, h)
+
+    def x_middle():
+        @pl.loop(3, 5)
         def _(i):
-            add_into(dwp.at[xx * 4 + i, c], sib_v.at[xx * 4 + i])
-
-    def side(h, dz):
-        if dz == 0:
-            return cols(h)
-        return pl.ds((0, 2560)[h], 1536)
-
-    def kept(dz):
-        return pl.ds(0, HALF if dz == 0 else 1536)
-
-    def far_x(h, p):
-        send(
-            xpart(2, 1, quarter(2 * h + p)), rel_v.at[h, 1, :, pl.ds(768 * p, 768)],
-            ("R", h, 1, p), (yp, ym)[h],
-        )
-
-    def near_x(s, dz, h):
-        dy, device = ((1, yp), (-1, ym))[s]
-        send(xpart(dy, dz, side(h, dz)), fin_v.at[s, dz, h, :, kept(dz)], ("F", s, dz, h), device)
-
-    def relay_x(dz):
-        for h, dy, source in ((0, 1, ym), (1, -1, yp)):
-            if dz == 0:
-                recv(rel_v.at[h, 0], ("R", h, 0), source)
-            else:
-                for p in range(2):
-                    recv(rel_v.at[h, 1, :, pl.ds(768 * p, 768)], ("R", h, 1, p), source)
-            add_into(xpart(dy, dz, side(h, dz)), rel_v.at[h, dz, :, kept(dz)])
-            near_x(h, dz, h)
+            x_term(i)
+
+        for dy in POSITION:
+            middle_x(dy)
+
+    def x_outer():
+        @pl.loop(0, 3)
+        def _(p):
+            for h in range(2):
+                x_term(p + 5 * h)
+                first = pl.multiple_of((p + 5 * h) * 512, 512)
+                pltpu.make_async_remote_copy(
+                    src_ref=xpart(2, 1, pl.ds(first, 512)),
+                    dst_ref=rel_v.at[h, 1, :, pl.ds(pl.multiple_of(p * 512, 512), 512)],
+                    send_sem=far_sem.at[p, h], recv_sem=recv_sem.at[far_key + 2 * p + h],
+                    device_id=(yp, ym)[h], device_id_type=MESH,
+                ).start()
 
     def middle_x(dy):
         send(xpart(dy, 1, MIDDLE), zb_v.at[POSITION[dy]], ("ZB", dy), mate)
@@ -407,12 +458,17 @@
         recv(zb_v.at[POSITION[dy]], ("ZB", dy), mate)
         add_into(xpart(dy, 0, MIDDLE), zb_v.at[POSITION[dy]])
 
-    def recv_near(s, dz, h):
-        recv(fin_v.at[s, dz, h, :, kept(dz)], ("F", s, dz, h), (ym, yp)[s])
-
-    up_units, down_units = (2, -1), (1, 0)
-    zs = {0: zh, 1: zq, 2: z2, -1: zn}
-
+    def recv_near(s, part, h):
+        recv(arrivals(fin_v, part, s, h), ("F", s, part, h), (ym, yp)[s])
+
+    def own_total(part, h):
+        return (
+            piece(0, part, h)[...].astype(F32)
+            + arrivals(fin_v, part, 0, h)[...].astype(F32)
+            + arrivals(fin_v, part, 1, h)[...].astype(F32)
+        )
+
+    up_units = (2, -1)
     def far_w(dz):
         if dz in up_units:
             send(wunit(x2, zs[dz]), xrel_v.at[zs[dz]], ("XR", dz), xp)
@@ -437,102 +493,137 @@
         recv(xfin_v.at[1, zs[dz]], ("XF", 1, dz), xp)
         add_two(wunit(x, zs[dz]), xfin_v.at[0, zs[dz]], xfin_v.at[1, zs[dz]])
 
+    top, bottom = pl.ds(0, 128), pl.ds(128, 128)
+
     def wz_half(zz, part):
         return dwp.at[x * 4 + zz, c, :, part]
 
     def mate_x(h):
-        part = xpart(0, 1, side(h, 1))
-        add_two(part, fin_v.at[0, 1, h, :, kept(1)], fin_v.at[1, 1, h, :, kept(1)])
-        send(part, zl_v.at[h], ("Z", h), mate)
-
-    for p in range(2):
-        for h in range(2):
-            x_term(0, 160, quarter(2 * h + p))
-            far_x(h, p)
-    x_term(0, SEQ, MIDDLE)
-    for dy in POSITION:
-        middle_x(dy)
-    w_term(x2)
-    send_sib(x2, 2)
-    for k in range(4):
-        x_term(160, 480, quarter(k))
-    near_x(0, 1, 1)
-    near_x(1, 1, 0)
-    recv_sib(x2, 2)
-    far_w(2)
-    far_w(1)
-    w_term(xq)
-    send_sib(xq, 1)
-    w_term(xn)
-    send_sib(xn, -1)
-    relay_x(1)
-    recv_sib(xq, 1)
-    recv_sib(xn, -1)
-    near_w(2)
-    w_term(x)
-    send_sib(x, 0)
-    near_w(1)
-    far_w(-1)
-    far_w(0)
-    recv_near(0, 1, 1)
-    recv_near(1, 1, 0)
-    add_middle(2)
-    send(xpart(2, 0, cols(0)), rel_v.at[0, 0], ("R", 0, 0), yp)
-    send(xpart(2, 0, cols(1)), rel_v.at[1, 0], ("R", 1, 0), ym)
-    recv_sib(x, 0)
-    sum_w(2)
-    send(wz_half(z2, top), zrel_v.at[0], ("ZR", 0), zp)
-    send(wz_half(z2, bottom), zrel_v.at[1], ("ZR", 1), zm)
-    recv_near(0, 1, 0)
-    mate_x(0)
-    recv_near(1, 1, 1)
-    mate_x(1)
-    add_middle(1)
-    add_middle(-1)
-    near_x(0, 0, 1)
-    near_x(1, 0, 0)
-    add_middle(0)
-    near_w(-1)
-    sum_w(1)
-    send(wz_half(zq, bottom), zfin_v.at[0, :, bottom], ("ZF", 0, 1), zp)
-    near_w(0)
-    sum_w(-1)
-    send(wz_half(zn, top), zfin_v.at[1, :, top], ("ZF", 1, 0), zm)
-    recv(zrel_v.at[0], ("ZR", 0), zm)
-    add_into(wz_half(zq, top), zrel_v.at[0])
-    send(wz_half(zq, top), zfin_v.at[0, :, top], ("ZF", 0, 0), zp)
-    recv(zrel_v.at[1], ("ZR", 1), zp)
-    add_into(wz_half(zn, bottom), zrel_v.at[1])
-    send(wz_half(zn, bottom), zfin_v.at[1, :, bottom], ("ZF", 1, 1), zm)
-    relay_x(0)
-    sum_w(0)
-
-    recv(zfin_v.at[0, :, bottom], ("ZF", 0, 1), zm)
-    recv(zfin_v.at[0, :, top], ("ZF", 0, 0), zm)
-    recv(zfin_v.at[1, :, top], ("ZF", 1, 0), zp)
-    recv(zfin_v.at[1, :, bottom], ("ZF", 1, 1), zp)
-    dw_out[...] = (
-        wunit(x, zh)[...].astype(F32) + zfin_v[0].astype(F32) + zfin_v[1].astype(F32)
-    )
-
-    for h in range(2):
+        recv_near(0, 1, h)
+        recv_near(1, 1, h)
+        add_rows(piece(0, 1, h), arrivals(fin_v, 1, 0, h), arrivals(fin_v, 1, 1, h))
+        send(piece(0, 1, h), zl_v.at[h], ("Z", h), mate)
+
+    def z_far():
+        send(wz_half(z2, top), zrel_v.at[0], ("ZR", 0), zp)
+        send(wz_half(z2, bottom), zrel_v.at[1], ("ZR", 1), zm)
+
+    def z_near(s, part, k):
+        zz, device = ((zq, zp), (zn, zm))[s]
+        send(wz_half(zz, part), zfin_v.at[s, :, part], ("ZF", s, k), device)
+
+    def z_relay(s):
+        zz, part, source = ((zq, top, zm), (zn, bottom, zp))[s]
+        recv(zrel_v.at[s], ("ZR", s), source)
+        add_into(wz_half(zz, part), zrel_v.at[s])
+        z_near(s, part, s)
+
+    def finish_x(h):
         recv(zl_v.at[h], ("Z", h), mate)
         recv_near(0, 0, h)
         recv_near(1, 0, h)
-        total = (
-            xpart(0, 0, cols(h))[...].astype(F32)
-            + fin_v[0, 0, h].astype(F32)
-            + fin_v[1, 0, h].astype(F32)
-        )
-        if h == 0:
-            dx_out[:, :1536] = (total[:, :1536] + zl_v[0].astype(F32)).astype(BF16)
-            dx_out[:, 1536:HALF] = total[:, 1536:].astype(BF16)
-        else:
-            dx_out[:, HALF:2560] = total[:, :512].astype(BF16)
-            dx_out[:, 2560:] = (total[:, 512:] + zl_v[1].astype(F32)).astype(BF16)
+        dx_out[:, side(h, 0)] = (own_total(0, h) + zl_v[h].astype(F32)).astype(BF16)
+
+    def finish_middle(h):
+        recv_near(0, 2, h)
+        recv_near(1, 2, h)
+        dx_out[:, side(h, 2)] = own_total(2, h).astype(BF16)
+
+    def finish_w():
+        recv(zfin_v.at[0, :, bottom], ("ZF", 0, 1), zm)
+        recv(zfin_v.at[0, :, top], ("ZF", 0, 0), zm)
+        recv(zfin_v.at[1, :, top], ("ZF", 1, 0), zp)
+        recv(zfin_v.at[1, :, bottom], ("ZF", 1, 1), zp)
+        for j in range(3):
+            total = (
+                dwp[x * 4 + zh, c, j].astype(F32)
+                + zfin_v[0, j].astype(F32)
+                + zfin_v[1, j].astype(F32)
+            )
+            dw_out[j] = total.T
+
+    x_outer()
+    gt[...] = gr[...].T
+    near_both(1)
+    x_middle()
+    w_terms(4)
+    w_terms(0)
+    w_terms(2)
+    w_sibling(2, 2)
+    w_sibling(-1, -1)
+    far_w(2)
+    w_terms(7)
+    relay_x(1, 0)
+    w_terms(6)
+    w_sibling(2, 1)
+    far_w(1)
+    w_terms(5)
+    w_sibling(2, -1)
+    w_sibling(0, 0)
+    relay_x(1, 1)
+    far_w(-1)
+    w_terms(1)
+    w_sibling(1, 2)
+    w_sibling(-1, 2)
+    w_sibling(1, -1)
+    w_sibling(1, 0)
+    near_w(2)
+    w_terms(3)
+    mate_x(0)
+    far_own(0)
+    w_sibling(0, 2)
+    w_sibling(2, 0)
+    mate_x(1)
+    w_sibling(-1, 1)
+    w_sibling(1, 1)
+    add_middle(2)
+    add_middle(-1)
+    add_middle(1)
+    near_w(-1)
+    sum_w(2)
+    far_own(2)
+    near_w(1)
+    relay_x(0, 1)
+    near_both(2)
+    w_sibling(-1, 0)
+    w_sibling(0, -1)
+    near_both(0)
+    relay_x(2, 0)
+    w_sibling(0, 1)
+    relay_x(2, 1)
+    far_w(0)
+    z_far()
+    sum_w(-1)
+    sum_w(1)
+    z_near(1, top, 0)
+    relay_x(0, 0)
+    z_near(0, bottom, 1)
+    near_w(0)
+    z_relay(1)
+    z_relay(0)
+    finish_x(1)
+    add_middle(0)
+    sum_w(0)
+    finish_middle(1)
+    finish_x(0)
+    finish_middle(0)
+    finish_w()
 
     for copy in sends:
         copy.wait_send()
+    for p in range(3):
+        for h in range(2):
+            block = rel_v.at[h, 1, :, pl.ds(512 * p, 512)]
+            pltpu.make_async_remote_copy(
+                src_ref=block, dst_ref=block, send_sem=far_sem.at[p, h],
+                recv_sem=recv_sem.at[far_key], device_id=yp, device_id_type=MESH,
+            ).wait_send()
+    for n in range(8):
+        for step in range(2):
+            pltpu.make_async_remote_copy(
+                src_ref=sib_v.at[0], dst_ref=sib_v.at[0], send_sem=sib_sem.at[n, step],
+                recv_sem=recv_sem.at[far_key], device_id=sibling, device_id_type=MESH,
+            ).wait_send()
     assert len(sends) <= N_SEND and len(keys) <= N_RECV
 
 
@@ -558,21 +649,24 @@
             pltpu.VMEM((3, 2, SEQ, HS), BF16),
             pltpu.VMEM((SEQ, 768), BF16),
             pltpu.VMEM((SEQ, 768), BF16),
+            pltpu.VMEM((768, SEQ), BF16),
             pltpu.VMEM((4, SEQ, HS), F32),
             pltpu.VMEM((SEQ, D), BF16),
-            pltpu.VMEM((16, 2, 3, 128, 256), BF16),
-            pltpu.VMEM((2, 2, 80, HALF), BF16),
-            pltpu.VMEM((2, 2, 2, 80, HALF), BF16),
+            pltpu.VMEM((16, 2, 3, 256, 128), BF16),
+            pltpu.VMEM((2, 3, 80, 1536), BF16),
+            pltpu.VMEM((2, 2, 3, 80, 1536), BF16),
             pltpu.VMEM((2, 80, 1536), BF16),
             pltpu.VMEM((4, 80, 1024), BF16),
-            pltpu.VMEM((16, 3, 128, 256), BF16),
-            pltpu.VMEM((4, 3, 128, 256), BF16),
-            pltpu.VMEM((2, 4, 3, 128, 256), BF16),
-            pltpu.VMEM((2, 3, 64, 256), BF16),
-            pltpu.VMEM((2, 3, 128, 256), BF16),
+            pltpu.VMEM((16, 3, 256, 128), BF16),
+            pltpu.VMEM((4, 3, 256, 128), BF16),
+            pltpu.VMEM((2, 4, 3, 256, 128), BF16),
+            pltpu.VMEM((2, 3, 128, 128), BF16),
+            pltpu.VMEM((2, 3, 256, 128), BF16),
             pltpu.SemaphoreType.DMA((N_SEND,)),
             pltpu.SemaphoreType.DMA((N_RECV,)),
             pltpu.SemaphoreType.DMA((5,)),
+            pltpu.SemaphoreType.DMA((3, 2)),
+            pltpu.SemaphoreType.DMA((8, 2)),
         ],
         compiler_params=pltpu.CompilerParams(
             collective_id=0, has_side_effects=True, vmem_limit_bytes=60 * 2**20

time: 113 us -> 112 us (level)
    pallas_call x1, Pallas kernels: 109 us -> 108 us  [shards(): pl.pallas_call(kernel, out_shape=(jax.ShapeDtypeStruct((80, D), BF16), ja...]
where the time goes in v4:
time: 112 us; the launch traced here: 111 us
  Pallas kernels  108 us (96%)
  local copies, waits for them, and re-layouts  2.77 us (2%)
    pallas_call x1, Pallas kernels, shards(): pl.pallas_call(kernel, out_shape=(jax.ShapeDtypeStruct((80, D), BF16), ja...  108 us
    unnamed x4, local copies, waits for them, and re-layouts  2.77 us

profile of v4, /device:TPU:1, one launch (start us, length us, event | category | flops | bytes accessed | tf_op | source)
XLA Modules:
  0.0 111.5 jit_solution(11588102079733532029)
XLA Ops:
  0.6 108.1 %mixer_backward.1 = (bf16[80,4096]{1,0:T(8,128)(2,1)}, f32[3,128,256]{2,1,0:T(8,128)}) custom-call(bf16[80,4096]{1,0:T(8,128)(2,1)} %x_in.1, bf16[3,128,256]{2,1,0:T(8,128)(2,1)} %w_in.1, bf16[640,256]{1,0:T(8,128)(2,1)} %up_in.1, f32[640,128]{1,0:T(8,128)} %constant.4.clone.cos_in, f32[640,128]{1,0:T(8,128)} %constant.5.clone.sin_in), custom_call_target="tpu_custom_call" | custom-call | tf_op jit(solution)/shard_map/mixer_backward/pallas_call | solution.py:634
  108.7 0.0 copy-start
  108.7 2.0 %copy.9 = bf16[80,4096]{1,0:T(8,128)(2,1)} copy(bf16[80,4096]{1,0:T(8,128)(2,1)} %get-tuple-element.4) | data formatting | bytes 1310720
  110.7 0.0 copy-done
  110.7 0.7 copy.10
Async XLA Ops:
  108.7 2.0 %copy-start = (f32[3,128,256]{2,1,0:T(8,128)S(1)}, f32[3,128,256]{2,1,0:T(8,128)}, u32[]{:S(2)}) copy-start(f32[3,128,256]{2,1,0:T(8,128)} %get-tuple-element.5) | copy-start | bytes 1179652

commit v5 on v4

--- a/solution.py
+++ b/solution.py
@@ -115,12 +115,11 @@
         pltpu.make_async_copy(cos_in, cosv, local_sem.at[3]),
         pltpu.make_async_copy(sin_in, sinv, local_sem.at[4]),
     ]
-    for copy in locals_:
-        copy.start()
-
     barrier = pltpu.get_barrier_semaphore()
     for device in everyone:
         pl.semaphore_signal(barrier, inc=1, device_id=device, device_id_type=MESH)
+    for copy in locals_:
+        copy.start()
     pl.semaphore_wait(barrier, len(everyone))
 
     top, bottom = pl.ds(0, 64), pl.ds(64, 64)
@@ -461,11 +460,11 @@
     def recv_near(s, part, h):
         recv(arrivals(fin_v, part, s, h), ("F", s, part, h), (ym, yp)[s])
 
-    def own_total(part, h):
+    def own_total(part, h, r):
         return (
-            piece(0, part, h)[...].astype(F32)
-            + arrivals(fin_v, part, 0, h)[...].astype(F32)
-            + arrivals(fin_v, part, 1, h)[...].astype(F32)
+            piece(0, part, h)[r].astype(F32)
+            + arrivals(fin_v, part, 0, h)[r].astype(F32)
+            + arrivals(fin_v, part, 1, h)[r].astype(F32)
         )
 
     up_units = (2, -1)
@@ -522,19 +521,29 @@
         recv(zl_v.at[h], ("Z", h), mate)
         recv_near(0, 0, h)
         recv_near(1, 0, h)
-        dx_out[:, side(h, 0)] = (own_total(0, h) + zl_v[h].astype(F32)).astype(BF16)
+
+        @pl.loop(0, 5)
+        def _(i):
+            r = pl.ds(pl.multiple_of(i * 16, 16), 16)
+            dx_out[r, side(h, 0)] = (own_total(0, h, r) + zl_v[h, r].astype(F32)).astype(BF16)
 
     def finish_middle(h):
         recv_near(0, 2, h)
         recv_near(1, 2, h)
-        dx_out[:, side(h, 2)] = own_total(2, h).astype(BF16)
+
+        @pl.loop(0, 5)
+        def _(i):
+            r = pl.ds(pl.multiple_of(i * 16, 16), 16)
+            dx_out[r, side(h, 2)] = own_total(2, h, r).astype(BF16)
 
     def finish_w():
         recv(zfin_v.at[0, :, bottom], ("ZF", 0, 1), zm)
         recv(zfin_v.at[0, :, top], ("ZF", 0, 0), zm)
         recv(zfin_v.at[1, :, top], ("ZF", 1, 0), zp)
         recv(zfin_v.at[1, :, bottom], ("ZF", 1, 1), zp)
-        for j in range(3):
+
+        @pl.loop(0, 3)
+        def _(j):
             total = (
                 dwp[x * 4 + zh, c, j].astype(F32)
                 + zfin_v[0, j].astype(F32)

time: 112 us -> 112 us (level)
  no operation moved by 1% of the time
where the time goes in v5:
time: 112 us
  Pallas kernels  108 us (96%)
  local copies, waits for them, and re-layouts  2.77 us (2%)
    pallas_call x1, Pallas kernels, shards(): pl.pallas_call(kernel, out_shape=(jax.ShapeDtypeStruct((80, D), BF16), ja...  108 us
    unnamed x4, local copies, waits for them, and re-layouts  2.77 us

profile of v5, /device:TPU:1, one launch (start us, length us, event | category | flops | bytes accessed | tf_op | source)
XLA Modules:
  0.0 111.6 jit_solution(504783379030736563)
XLA Ops:
  0.6 108.2 %mixer_backward.1 = (bf16[80,4096]{1,0:T(8,128)(2,1)}, f32[3,128,256]{2,1,0:T(8,128)}) custom-call(bf16[80,4096]{1,0:T(8,128)(2,1)} %x_in.1, bf16[3,128,256]{2,1,0:T(8,128)(2,1)} %w_in.1, bf16[640,256]{1,0:T(8,128)(2,1)} %up_in.1, f32[640,128]{1,0:T(8,128)} %constant.4.clone.cos_in, f32[640,128]{1,0:T(8,128)} %constant.5.clone.sin_in), custom_call_target="tpu_custom_call" | custom-call | tf_op jit(solution)/shard_map/mixer_backward/pallas_call | solution.py:643
  108.8 0.0 copy-start
  108.8 2.0 %copy.9 = bf16[80,4096]{1,0:T(8,128)(2,1)} copy(bf16[80,4096]{1,0:T(8,128)(2,1)} %get-tuple-element.4) | data formatting | bytes 1310720
  110.9 0.0 copy-done
  110.9 0.7 copy.10
Async XLA Ops:
  108.8 2.0 %copy-start = (f32[3,128,256]{2,1,0:T(8,128)S(1)}, f32[3,128,256]{2,1,0:T(8,128)}, u32[]{:S(2)}) copy-start(f32[3,128,256]{2,1,0:T(8,128)} %get-tuple-element.5) | copy-start | bytes 1179652
